TPU v7x, 768 devices: a whole 4x8x12 slice. The times are simulated.
768 devices in a mesh: dp: 96 (over x, z, core), tensor: 8 (over y).
Axes of the slice: x: 4, y: 8, z: 12, core: 2. Of those that a mesh axis runs over, the one named last changes fastest.
Arguments:
- tokens: bfloat16 [12288, 3584], P('dp', 'tensor'), may hold values from -6 to 6
- cotangent: bfloat16 [12288, 3584], P('dp', 'tensor'), may hold values from -6 to 6
- expert_ids: int32 [12288, 2], P('dp'), may hold values from 0 to 95, all different within a row; in each aligned block of 128 rows (0 to 127, 128 to 255, ...) at most 3 rows name the same one
- route_probs: float32 [12288, 2], P('dp'), may hold values from 0.05 to 1
- up_weight: bfloat16 [96, 3584, 2432], P('dp', 'tensor'), may hold values from -0.09375 to 0.09375
- down_weight: bfloat16 [96, 2432, 3584], P('dp', None, 'tensor'), may hold values from -0.125 to 0.125
Outputs:
- mixed: bfloat16 [12288, 3584], P('dp', 'tensor')
- input_grad: bfloat16 [12288, 3584], P('dp', 'tensor')
- prob_grad: float32 [12288, 2], P('dp')
Inputs may be any that keep to these rules, and one draw needn't show every extreme that they name: `expert_ids`: each row names two different experts. Among the rows of one index of dp (aligned blocks of 128 rows), no expert is named more than 3 times, a bound that some block reaches.
All inputs are finite; a program needn't handle non-finite values.
Results may differ from a plain program's by a relative error of at most 0.024.
Values may be sent and summed in bfloat16 or wider, within the bound.
No kernel may reach another device: no remote copies, remote signals or barrier semaphores. Data moves between devices by JAX's collectives and lax.ppermute only.
A program may use at most 64 MiB of HBM per device.

v0:
```python
import jax
import jax.numpy as jnp
from jax import lax
from jax.sharding import PartitionSpec as P


def hidden_share(partial_value):
    return lax.psum_scatter(
        partial_value.astype(jnp.bfloat16), "tensor", scatter_dimension=2, tiled=True
    ).astype(jnp.float32)


def hidden_whole(pieces):
    return lax.all_gather(pieces, "tensor", axis=2, tiled=True)


def route_out(block):
    return lax.all_to_all(block, "dp", split_axis=0, concat_axis=0, tiled=True)


def route_back(block):
    return lax.all_to_all(block, "dp", split_axis=0, concat_axis=0, tiled=True)


def expert_forward(rows_in, up_local, down_local):
    row_block = rows_in.reshape(-1, rows_in.shape[2])
    partial_value = jnp.dot(row_block, up_local, preferred_element_type=jnp.float32)
    up_sum = hidden_share(partial_value[:, None, :])[:, 0]
    hidden = jax.nn.silu(up_sum).astype(jnp.bfloat16)
    hidden_full = hidden_whole(hidden[:, None, :])[:, 0]
    expert_out = jnp.dot(hidden_full, down_local, preferred_element_type=jnp.float32).astype(
        jnp.bfloat16
    )
    return (expert_out.reshape(rows_in.shape), up_sum)


def expert_backward(grads_in, up_sum, up_local, down_local):
    grad_rows = grads_in.reshape(-1, grads_in.shape[2])
    contract = (((1,), (1,)), ((), ()))
    partial_value = lax.dot_general(
        grad_rows, down_local, contract, preferred_element_type=jnp.float32
    )
    hidden_grad = hidden_share(partial_value[:, None, :])[:, 0]
    up_sigmoid = jax.nn.sigmoid(up_sum)
    up_grad = (hidden_grad * up_sigmoid * (1.0 + up_sum * (1.0 - up_sigmoid))).astype(jnp.bfloat16)
    joined = hidden_whole(up_grad[:, None, :])[:, 0]
    input_part = lax.dot_general(joined, up_local, contract, preferred_element_type=jnp.float32)
    return input_part.astype(jnp.bfloat16).reshape(grads_in.shape)


def per_device(tokens, cotangent, expert_ids, route_probs, up_weight, down_weight):
    tok_rows = tokens.shape[0]
    feat_local = tokens.shape[1]
    dp_count = lax.axis_size("dp")
    expert_count = dp_count * up_weight.shape[0]
    capacity = max(2, (2 * tok_rows + dp_count - 1) // dp_count)
    slot_count = expert_count * capacity
    onehot = (
        expert_ids.reshape(-1)[:, None] == jnp.arange(expert_count, dtype=jnp.int32)[None, :]
    ).astype(jnp.int32)
    rank_table = jnp.cumsum(onehot, axis=0) - 1
    slot_index = jnp.sum(onehot * rank_table, axis=1).reshape(tok_rows, 2)
    flat_slot = expert_ids * capacity + slot_index
    lane_index = jnp.arange(slot_count, dtype=jnp.int32)[None, :]
    pick_first = (flat_slot[:, 0:1] == lane_index).astype(jnp.float32)
    pick_second = (flat_slot[:, 1:2] == lane_index).astype(jnp.float32)
    route_matrix = pick_first + pick_second
    weighted = pick_first * route_probs[:, 0:1] + pick_second * route_probs[:, 1:2]
    cot_float = cotangent.astype(jnp.float32)
    send_rows = jnp.dot(
        route_matrix.T.astype(jnp.bfloat16), tokens, preferred_element_type=jnp.float32
    )
    send_rows = send_rows.astype(jnp.bfloat16).reshape(expert_count, capacity, feat_local)
    send_grads = jnp.dot(weighted.T, cot_float, precision=lax.Precision.HIGHEST)
    send_grads = send_grads.astype(jnp.bfloat16).reshape(expert_count, capacity, feat_local)
    up_local = up_weight[0]
    down_local = down_weight[0]
    rows_in = route_out(send_rows)
    expert_out, saved = expert_forward(rows_in, up_local, down_local)
    out_back = route_back(expert_out)
    grads_in = route_out(send_grads)
    input_part = expert_backward(grads_in, saved, up_local, down_local)
    grad_back = route_back(input_part)
    out_flat = out_back.reshape(slot_count, feat_local).astype(jnp.float32)
    grad_flat = grad_back.reshape(slot_count, feat_local).astype(jnp.float32)
    mixed = jnp.dot(weighted, out_flat, precision=lax.Precision.HIGHEST).astype(jnp.bfloat16)
    input_grad = jnp.dot(route_matrix, grad_flat, precision=lax.Precision.HIGHEST).astype(
        jnp.bfloat16
    )
    first = jnp.dot(pick_first, out_flat, precision=lax.Precision.HIGHEST)
    second = jnp.dot(pick_second, out_flat, precision=lax.Precision.HIGHEST)
    partial_scores = jnp.stack(
        [jnp.sum(cot_float * first, axis=1), jnp.sum(cot_float * second, axis=1)], axis=1
    )
    prob_grad = lax.psum(partial_scores, "tensor")
    return (mixed, input_grad, prob_grad)


def solution(mesh):
    return jax.shard_map(
        per_device,
        mesh=mesh,
        in_specs=(
            P("dp", "tensor"),
            P("dp", "tensor"),
            P("dp", None),
            P("dp", None),
            P("dp", "tensor", None),
            P("dp", None, "tensor"),
        ),
        out_specs=(P("dp", "tensor"), P("dp", "tensor"), P("dp", None)),
        check_vma=False,
    )
```

profile of v0, /device:TPU:1, one launch (start us, length us, event | category | flops | bytes accessed | tf_op | source)
XLA Modules:
  0.0 330.5 jit_solution(8243217838577108760)
XLA Ops:
  11.1 1.5 convolution_convert_fusion.2
  12.8 41.6 %all_to_all.20 = bf16[96,3,448]{2,1,0:T(4,128)(2,1)S(1)} all-to-all(bf16[96,3,448]{2,1,0:T(4,128)(2,1)S(1)} %reshape.60), channel_id=1, replica_groups=mesh['dp'=96,'tensor'=8] {'dp'}, dimensions={0} | all-to-all | bytes 516096 | tf_op jit(solution)/shard_map/all_to_all | solution.py:18
  54.6 2.0 fusion.1
  56.7 8.6 %copy.45 = bf16[288,1,2432]{0,1,2:T(2,128)(2,1)} copy(bf16[288,1,2432]{2,0,1:T(8,128)(2,1)} %fusion.1) | data formatting | bytes 2801664
  65.2 3.7 %copy.53 = bf16[2432,1,288]{2,0,1:T(8,128)(2,1)} copy(bf16[2432,1,288]{2,1,0:T(2,128)(2,1)} %bitcast.75) | data formatting | bytes 2801664
  69.4 28.5 %all_to_all.21 = bf16[96,3,448]{2,1,0:T(4,128)(2,1)S(1)} all-to-all(bf16[96,3,448]{2,1,0:T(4,128)(2,1)S(1)} %reshape.56), channel_id=1, replica_groups=mesh['dp'=96,'tensor'=8] {'dp'}, dimensions={0} | all-to-all | bytes 516096 | tf_op jit(solution)/shard_map/all_to_all | solution.py:18
  98.2 3.7 %fusion = bf16[288,1,2432]{2,0,1:T(8,128)(2,1)} fusion(bf16[288,448]{1,0:T(8,128)(2,1)S(1)} %reshape.57, bf16[1,448,2432]{2,1,0:T(8,128)(2,1)} %param.10), kind=kOutput, calls=%fused_computation.2 | convolution fusion | flops 628273152 | bytes 3837952 | tf_op jit(solution)/shard_map/dot_general | solution.py:27
  101.9 8.6 %copy.43 = bf16[288,1,2432]{0,1,2:T(2,128)(2,1)} copy(bf16[288,1,2432]{2,0,1:T(8,128)(2,1)} %fusion) | data formatting | bytes 2801664
  110.5 3.6 %copy.54 = bf16[2432,1,288]{2,0,1:T(8,128)(2,1)} copy(bf16[2432,1,288]{2,1,0:T(2,128)(2,1)} %bitcast.76) | data formatting | bytes 2801664
  116.2 38.7 %reduce-scatter.7.cloned.1.call-done = bf16[304,288]{1,0:T(8,128)(2,1)} async-done(((bf16[2432,288]{1,0:T(8,128)(2,1)}), bf16[304,288]{1,0:T(8,128)(2,1)}) %reduce-scatter.7.cloned.1.call-update) | async-done | bytes 175120
  157.1 1.2 copy.39
  158.4 1.3 copy.41
  159.7 57.5 %all-gather.3.cloned.1.call-done = bf16[288,1,2432]{0,1,2:T(2,128)(2,1)} async-done(((bf16[288,1,304]{0,1,2:T(2,128)(2,1)}), bf16[288,1,2432]{0,1,2:T(2,128)(2,1)}) %all-gather.3.cloned.1.call-update) | async-done | bytes 1400848 | tf_op jit(solution)/shard_map/all_gather | solution.py:14
  217.2 8.5 %copy.40 = bf16[288,1,2432]{2,0,1:T(8,128)(2,1)} copy(bf16[288,1,2432]{0,1,2:T(2,128)(2,1)} %all-gather.3.cloned.1.call-done) | data formatting | bytes 2801664 | tf_op jit(solution)/shard_map/all_gather | solution.py:14
  225.7 2.3 fusion.15
  228.9 14.2 %all-to-all-start.1 = ((bf16[96,3,448]{2,1,0:T(4,128)(2,1)}), bf16[96,3,448]{2,1,0:T(4,128)(2,1)S(1)}, u32[]{:S(2)}, u32[]{:S(2)}) async-start(bf16[96,3,448]{2,1,0:T(4,128)(2,1)} %reshape.58), calls=%async_computation.1 | async-start | bytes 786432 | tf_op jit(solution)/shard_map/all_to_all | solution.py:22
  243.1 31.0 %all-gather.5.cloned.1.call-done = bf16[288,1,2432]{0,1,2:T(2,128)(2,1)} async-done(((bf16[288,1,304]{0,1,2:T(2,128)(2,1)}), bf16[288,1,2432]{0,1,2:T(2,128)(2,1)}) %all-gather.5.cloned.1.call-update) | async-done | bytes 1400848 | tf_op jit(solution)/shard_map/all_gather | solution.py:14
  274.1 8.4 %copy.42 = bf16[288,1,2432]{2,0,1:T(8,128)(2,1)} copy(bf16[288,1,2432]{0,1,2:T(2,128)(2,1)} %all-gather.5.cloned.1.call-done) | data formatting | bytes 2801664 | tf_op jit(solution)/shard_map/all_gather | solution.py:14
  282.5 3.0 fusion.10
  286.5 14.2 %all-to-all-start.3 = ((bf16[96,3,448]{2,1,0:T(4,128)(2,1)}), bf16[96,3,448]{2,1,0:T(4,128)(2,1)S(1)}, u32[]{:S(2)}, u32[]{:S(2)}) async-start(bf16[96,3,448]{2,1,0:T(4,128)(2,1)} %reshape.62), calls=%async_computation.3 | async-start | bytes 786432 | tf_op jit(solution)/shard_map/all_to_all | solution.py:22
  301.7 13.6 %psum.7 = f32[128,2]{0,1:T(2,128)} all-reduce(f32[128,2]{0,1:T(2,128)S(1)} %pad_maximum_fusion), channel_id=1, replica_groups=mesh['dp'=96,'tensor'=8] {'tensor'}, use_global_device_ids=true, to_apply=%region_7.8 | all-reduce | flops 256 | bytes 2048 | tf_op jit(solution)/shard_map/psum | solution.py:95
  315.2 1.3 convolution_convert_fusion.5
  316.5 5.9 %all-to-all-done.3 = bf16[96,3,448]{2,1,0:T(4,128)(2,1)S(1)} async-done(((bf16[96,3,448]{2,1,0:T(4,128)(2,1)}), bf16[96,3,448]{2,1,0:T(4,128)(2,1)S(1)}, u32[]{:S(2)}, u32[]{:S(2)}) %all-to-all-start.3) | async-done | bytes 258080 | tf_op jit(solution)/shard_map/all_to_all | solution.py:22
  322.7 1.3 convolution_convert_fusion.4
  (47 shorter events, 12.5 us)
Async XLA Ops:
  7.2 47.5 %copy-start = (bf16[1,2432,448]{1,2,0:T(8,128)(2,1)S(1)}, bf16[1,2432,448]{1,2,0:T(8,128)(2,1)}, u32[]{:S(2)}) copy-start(bf16[1,2432,448]{1,2,0:T(8,128)(2,1)} %param.11) | copy-start | bytes 6537220
  7.2 107.0 %reduce-scatter.9.cloned.1.call-start = ((), (), s32[]{:S(2)}) async-start(), calls=%async_computation.9 | async-start | bytes 2101248
  65.2 3.7 %copy-start.1 = (bf16[128,448]{0,1:T(8,128)(2,1)S(1)}, bf16[128,448]{0,1:T(8,128)(2,1)}, u32[]{:S(2)}) copy-start(bf16[128,448]{0,1:T(8,128)(2,1)} %param.6) | copy-start | bytes 344068
  68.9 85.9 %reduce-scatter.7.cloned.1.call-start = ((), (), s32[]{:S(2)}) async-start(), calls=%async_computation.8 | async-start | bytes 2101248
  114.1 103.1 %all-gather.3.cloned.1.call-start = ((), (), s32[]{:S(2)}) async-start(), calls=%async_computation.6 | async-start | bytes 4202496 | tf_op jit(solution)/shard_map/all_gather | solution.py:14
  158.4 115.7 %all-gather.5.cloned.1.call-start = ((), (), s32[]{:S(2)}) async-start(), calls=%async_computation.7 | async-start | bytes 4202496 | tf_op jit(solution)/shard_map/all_gather | solution.py:14
  228.9 57.6 %all-to-all-start.1 = ((bf16[96,3,448]{2,1,0:T(4,128)(2,1)}), bf16[96,3,448]{2,1,0:T(4,128)(2,1)S(1)}, u32[]{:S(2)}, u32[]{:S(2)}) async-start(bf16[96,3,448]{2,1,0:T(4,128)(2,1)} %reshape.58), calls=%async_computation.1 | async-start | bytes 786432 | tf_op jit(solution)/shard_map/all_to_all | solution.py:22
  282.5 18.4 %copy-start.2 = (bf16[128,448]{0,1:T(8,128)(2,1)S(1)}, bf16[128,448]{0,1:T(8,128)(2,1)}, u32[]{:S(2)}) copy-start(bf16[128,448]{0,1:T(8,128)(2,1)} %param.7) | copy-start | bytes 344068
  286.5 35.9 %all-to-all-start.3 = ((bf16[96,3,448]{2,1,0:T(4,128)(2,1)}), bf16[96,3,448]{2,1,0:T(4,128)(2,1)S(1)}, u32[]{:S(2)}, u32[]{:S(2)}) async-start(bf16[96,3,448]{2,1,0:T(4,128)(2,1)} %reshape.62), calls=%async_computation.3 | async-start | bytes 786432 | tf_op jit(solution)/shard_map/all_to_all | solution.py:22
Sparse Core Ops, SparseCore 0:
  69.1 36.8 reduce-scatter.8
  114.2 40.5 reduce-scatter.6
  158.5 58.6 all-gather.2
  219.4 54.6 all-gather.4
where the time goes:
time: 332 us; the launch traced here: 330 us
  waiting for transfers between devices  133 us (40%)
  blocking collectives  83.6 us (25%)
  local copies, waits for them, and re-layouts  53.4 us (16%)
  starting transfers between devices  28.5 us (9%)
  matrix products  16.1 us (5%)
  between operations  13.9 us (4%)
    all_gather x2, waiting for transfers between devices, hidden_whole(): return lax.all_gather(pieces, 'tensor', axis=2, tiled=True)  88.5 us
    all_to_all x2, blocking collectives, route_out(): return lax.all_to_all(block, 'dp', split_axis=0, concat_axis=0, tiled=True)  70.1 us
    unnamed x6, waiting for transfers between devices  38.7 us
    unnamed x15, local copies, waits for them, and re-layouts  29.4 us
    all_to_all x2, starting transfers between devices, route_back(): return lax.all_to_all(block, 'dp', split_axis=0, concat_axis=0, tiled=True)  28.4 us
    all_gather x2, local copies, waits for them, and re-layouts, hidden_whole(): return lax.all_gather(pieces, 'tensor', axis=2, tiled=True)  16.9 us
    psum x1, blocking collectives, per_device(): prob_grad = lax.psum(partial_scores, 'tensor')  13.6 us
  transfers between devices with their start and end apart: 6, of which 4 were waited for; matrix products, arithmetic and copies ran while one was open for 14% of the time, Pallas kernels for 0%

commit v1 on v0

v1 whole, which is shorter than its diff:
```python
import jax
import jax.numpy as jnp
from jax import lax
from jax.experimental import pallas as pl
from jax.experimental.pallas import tpu as pltpu
from jax.sharding import PartitionSpec as P

CAP = 3
LANES = 128
BLOCK = 24
ROWS = 320
F32 = jnp.float32
BF16 = jnp.bfloat16
MIB = 1024 * 1024


def params(mib):
    return pltpu.CompilerParams(vmem_limit_bytes=mib * MIB)


def one_hots(ids_ref, experts):
    tokens = ids_ref.shape[1]
    expert = lax.broadcasted_iota(jnp.int32, (experts, tokens), 0)
    named = [(ids_ref[k : k + 1, :] == expert).astype(F32) for k in range(2)]
    before = lax.broadcasted_iota(jnp.int32, (tokens, tokens), 0)
    after = lax.broadcasted_iota(jnp.int32, (tokens, tokens), 1)
    earlier = (before < after).astype(F32).astype(BF16)
    slot = jnp.dot((named[0] + named[1]).astype(BF16), earlier, preferred_element_type=F32)
    return named, slot


def tile_of(first, second, j):
    if j < 3:
        return first[:, j * LANES : (j + 1) * LANES]
    if j < 6:
        return second[:, (j - 3) * LANES : (j - 2) * LANES]
    return jnp.concatenate([first[:, 3 * LANES :], second[:, 3 * LANES :]], axis=1)


def pair_of(tiles):
    half = LANES // 2
    first = jnp.concatenate(tiles[0:3] + [tiles[6][:, :half]], axis=1)
    second = jnp.concatenate(tiles[3:6] + [tiles[6][:, half:]], axis=1)
    return first, second


def dispatch_kernel(ids_ref, probs_ref, tok_ref, cot_ref, out_ref, scratch):
    experts = out_ref.shape[0] // BLOCK
    named, slot = one_hots(ids_ref, experts)
    either = named[0] + named[1]
    weight = named[0] * probs_ref[0:1, :] + named[1] * probs_ref[1:2, :]
    across = (((1,), (1,)), ((), ()))
    for s in range(CAP):
        here = (slot == s).astype(F32)
        pick = (either * here).astype(BF16)
        rows = lax.dot_general(pick, tok_ref[...], across, preferred_element_type=F32)
        grads = lax.dot_general(pick, cot_ref[...], across, preferred_element_type=F32)
        grads = grads * jnp.sum(weight * here, axis=1, keepdims=True)
        for j in range(7):
            scratch[pl.ds(s * 7 + j, experts, stride=BLOCK), :] = tile_of(rows, grads, j)
    for r in range(7 * CAP, BLOCK):
        scratch[pl.ds(r, experts, stride=BLOCK), :] = jnp.zeros((experts, LANES), F32)
    out_ref[...] = scratch[...].astype(BF16)


def up_kernel(block_ref, up_ref, down_ref, out_ref, scratch):
    sources = block_ref.shape[0] // BLOCK
    hidden = up_ref.shape[1]
    scratch[...] = block_ref[...].astype(F32)
    rows, grads = [], []
    for s in range(CAP):
        tiles = [scratch[pl.ds(s * 7 + j, sources, stride=BLOCK), :] for j in range(7)]
        first, second = pair_of(tiles)
        rows.append(first)
        grads.append(second)
    pad = jnp.zeros((ROWS - CAP * sources, up_ref.shape[0]), F32)
    rows = jnp.concatenate(rows + [pad], axis=0).astype(BF16)
    grads = jnp.concatenate(grads + [pad], axis=0).astype(BF16)
    for left, weight, base in ((rows, up_ref, 0), (grads, down_ref, hidden)):
        for at in range(0, hidden, 512):
            to = min(at + 512, hidden)
            out_ref[:, base + at : base + to] = jnp.dot(
                left, weight[:, at:to], preferred_element_type=F32
            ).astype(BF16)


def middle_kernel(sum_ref, out_ref):
    hidden = sum_ref.shape[1] // 2
    up_sum = sum_ref[:, :hidden].astype(F32)
    grad = sum_ref[:, hidden:].astype(F32)
    sigmoid = 1.0 / (1.0 + jnp.exp(-up_sum))
    act = (up_sum * sigmoid).astype(BF16)
    out_ref[:, :hidden] = act
    out_ref[:, hidden : 2 * hidden] = (
        grad * sigmoid * (1.0 + up_sum * (1.0 - sigmoid))
    ).astype(BF16)
    score = jnp.sum(act.astype(F32) * grad, axis=1, keepdims=True)
    high = score.astype(BF16).astype(F32)
    lane = lax.broadcasted_iota(jnp.int32, (sum_ref.shape[0], LANES), 1)
    out_ref[:, 2 * hidden :] = jnp.where(
        lane == 0, high, jnp.where(lane == 1, score - high, 0.0)
    ).astype(BF16)


def down_kernel(join_ref, up_ref, down_ref, out_ref, scratch):
    sources = out_ref.shape[0] // BLOCK
    hidden = up_ref.shape[1]
    across = (((1,), (1,)), ((), ()))
    out = lax.dot_general(
        join_ref[:, :hidden], down_ref[...], across, preferred_element_type=F32
    )
    part = lax.dot_general(
        join_ref[:, hidden : 2 * hidden], up_ref[...], across, preferred_element_type=F32
    )
    score = join_ref[:, 2 * hidden :].astype(F32)
    for s in range(CAP):
        rows = slice(s * sources, (s + 1) * sources)
        for j in range(7):
            scratch[pl.ds(s * 7 + j, sources, stride=BLOCK), :] = tile_of(out[rows], part[rows], j)
        scratch[pl.ds(7 * CAP + s, sources, stride=BLOCK), :] = score[rows]
    out_ref[...] = scratch[...].astype(BF16)


def combine_kernel(ids_ref, probs_ref, block_ref, mixed_ref, grad_ref, score_ref, scratch):
    experts = block_ref.shape[0] // BLOCK
    named, slot = one_hots(ids_ref, experts)
    scratch[...] = block_ref[...].astype(F32)
    along = (((0,), (0,)), ((), ()))
    outs, parts, picks = [], [], []
    scores = [jnp.zeros((1, ids_ref.shape[1]), F32) for _ in range(2)]
    for s in range(CAP):
        here = (slot == s).astype(F32)
        tiles = [scratch[pl.ds(s * 7 + j, experts, stride=BLOCK), :] for j in range(7)]
        first, second = pair_of(tiles)
        outs.append(first)
        parts.append(second)
        picks.append(jnp.concatenate([named[0] * here, named[1] * here], axis=1))
        tail = scratch[pl.ds(7 * CAP + s, experts, stride=BLOCK), :]
        value = tail[:, 0:1] + tail[:, 1:2]
        for k in range(2):
            scores[k] += jnp.sum(named[k] * here * value, axis=0, keepdims=True)
    outs = jnp.concatenate(outs, axis=0).astype(BF16)
    parts = jnp.concatenate(parts, axis=0).astype(BF16)
    picks = jnp.concatenate(picks, axis=0)
    tokens = ids_ref.shape[1]
    either = (picks[:, :tokens] + picks[:, tokens:]).astype(BF16)
    got = lax.dot_general(outs, picks.astype(BF16), along, preferred_element_type=F32)
    mixed_ref[...] = (
        got[:, :tokens] * probs_ref[0:1, :] + got[:, tokens:] * probs_ref[1:2, :]
    ).astype(BF16)
    grad_ref[...] = lax.dot_general(parts, either, along, preferred_element_type=F32).astype(BF16)
    score_ref[...] = jnp.concatenate(scores, axis=0) / probs_ref[...]


def exchange(block, experts):
    block = block.reshape(experts, BLOCK, LANES)
    block = lax.all_to_all(block, "dp", split_axis=0, concat_axis=0, tiled=True)
    return block.reshape(experts * BLOCK, LANES)


def per_device(tokens, cotangent, expert_ids, route_probs, up_weight, down_weight):
    count, feat = tokens.shape
    experts = lax.axis_size("dp")
    hidden = up_weight.shape[2]
    ids, probs = expert_ids.T, route_probs.T
    up, down = up_weight[0], down_weight[0].T
    packed = jax.ShapeDtypeStruct((experts * BLOCK, LANES), BF16)
    stage = [pltpu.VMEM((experts * BLOCK, LANES), F32)]
    send = pl.pallas_call(
        dispatch_kernel, out_shape=packed, scratch_shapes=stage, compiler_params=params(16)
    )(ids, probs, tokens.T, cotangent.T)
    partial = pl.pallas_call(
        up_kernel,
        out_shape=jax.ShapeDtypeStruct((ROWS, 2 * hidden), BF16),
        scratch_shapes=stage,
        compiler_params=params(24),
    )(exchange(send, experts), up, down)
    share = lax.psum_scatter(partial, "tensor", scatter_dimension=0, tiled=True)
    middle = pl.pallas_call(
        middle_kernel,
        out_shape=jax.ShapeDtypeStruct((share.shape[0], 2 * hidden + LANES), BF16),
        compiler_params=params(16),
    )(share)
    joined = lax.all_gather(middle, "tensor", axis=0, tiled=True)
    back = pl.pallas_call(
        down_kernel, out_shape=packed, scratch_shapes=stage, compiler_params=params(24)
    )(joined, up, down)
    mixed, input_grad, prob_grad = pl.pallas_call(
        combine_kernel,
        out_shape=(
            jax.ShapeDtypeStruct((feat, count), BF16),
            jax.ShapeDtypeStruct((feat, count), BF16),
            jax.ShapeDtypeStruct((2, count), F32),
        ),
        scratch_shapes=stage,
        compiler_params=params(16),
    )(ids, probs, exchange(back, experts))
    return mixed.T, input_grad.T, prob_grad.T


def solution(mesh):
    return jax.shard_map(
        per_device,
        mesh=mesh,
        in_specs=(
            P("dp", "tensor"),
            P("dp", "tensor"),
            P("dp", None),
            P("dp", None),
            P("dp", "tensor", None),
            P("dp", None, "tensor"),
        ),
        out_specs=(P("dp", "tensor"), P("dp", "tensor"), P("dp", None)),
        check_vma=False,
    )
```

time: 332 us -> 220 us (0.66)
  local copies, waits for them, and re-layouts: 53.4 us -> 10.9 us
  waiting for transfers between devices: 133 us -> 96.9 us
  starting transfers between devices: 28.5 us -> 0.08 us
  matrix products: 16.1 us -> 0 us
  Pallas kernels: 0 us -> 8.54 us
  blocking collectives: 83.6 us -> 88.7 us
    reduce_scatter x0 -> x1, waiting for transfers between devices: none -> 43.8 us  [per_device(): share = lax.psum_scatter(partial, 'tensor', scatter_dimension=0, tiled=True)]
    unnamed x6 -> x2, waiting for transfers between devices: 38.7 us -> 0.03 us
    all_gather x2 -> x1, waiting for transfers between devices: 88.5 us -> 53.1 us  [per_device(): joined = lax.all_gather(middle, 'tensor', axis=0, tiled=True)]
    all_to_all x2 -> x0, starting transfers between devices: 28.4 us -> none  [route_back(): return lax.all_to_all(block, 'dp', split_axis=0, concat_axis=0, tiled=True)]
    all_to_all x2, blocking collectives: 70.1 us -> 88.7 us  [exchange(): block = lax.all_to_all(block, 'dp', split_axis=0, concat_axis=0, tiled=True)]
    unnamed x15 -> x24, local copies, waits for them, and re-layouts: 29.4 us -> 10.9 us
    all_gather x2 -> x0, local copies, waits for them, and re-layouts: 16.9 us -> none  [hidden_whole(): return lax.all_gather(pieces, 'tensor', axis=2, tiled=True)]
    dot_general x10 -> x0, matrix products: 16.1 us -> none  [the longest x1 3.7 us: expert_forward(): jnp.dot(row_block, up_local, preferred_element_type=jnp.float32)]
  transfers between devices with their start and end apart: 6 -> 2, of which waited for: 4 -> 2; matrix products, arithmetic and copies ran while one was open for 14% -> 0% of each run, Pallas kernels for 0% -> 0%
where the time goes in v1:
time: 220 us; the launch traced here: 219 us
  waiting for transfers between devices  96.9 us (44%)
  blocking collectives  88.7 us (40%)
  between operations  14.1 us (6%)
  local copies, waits for them, and re-layouts  10.9 us (5%)
  Pallas kernels  8.54 us (4%)
    all_to_all x2, blocking collectives, exchange(): block = lax.all_to_all(block, 'dp', split_axis=0, concat_axis=0, tiled=True)  88.7 us
    all_gather x1, waiting for transfers between devices, per_device(): joined = lax.all_gather(middle, 'tensor', axis=0, tiled=True)  53.1 us
    reduce_scatter x1, waiting for transfers between devices, per_device(): share = lax.psum_scatter(partial, 'tensor', scatter_dimension=0, tiled=True)  43.8 us
    unnamed x24, local copies, waits for them, and re-layouts  10.9 us
  transfers between devices with their start and end apart: 2, of which 2 were waited for; matrix products, arithmetic and copies ran while one was open for 0% of the time, Pallas kernels for 0%

profile of v1, /device:TPU:1, one launch (start us, length us, event | category | flops | bytes accessed | tf_op | source)
XLA Modules:
  0.0 219.2 jit_solution(10543174012377910292)
XLA Ops:
  7.2 0.0 reduce-scatter.2.cloned.1.call-start
  7.2 0.0 copy-start.6
  7.2 0.9 copy-done.6
  8.1 0.9 copy-done.7
  9.0 0.7 copy-done.8
  9.7 0.7 copy-done.10
  10.4 0.7 shard_map.85
  11.0 47.1 %all_to_all.10 = bf16[96,24,128]{2,1,0:T(8,128)(2,1)S(1)} all-to-all(bf16[96,24,128]{2,1,0:T(8,128)(2,1)S(1)} %bitcast.20), channel_id=1, replica_groups=mesh['dp'=96,'tensor'=8] {'dp'}, dimensions={0} | all-to-all | bytes 1179648 | tf_op jit(solution)/shard_map/all_to_all | solution.py:157
  58.2 1.6 copy-done
  59.8 1.6 copy-done.2
  61.4 3.5 %shard_map.86 = bf16[320,4864]{1,0:T(8,128)(2,1)} custom-call(bf16[2304,128]{1,0:T(8,128)(2,1)S(1)} %bitcast.21, bf16[448,2432]{1,0:T(8,128)(2,1)S(1)} %bitcast.15, bf16[448,2432]{1,0:T(8,128)(2,1)S(1)} %bitcast.17), custom_call_target="tpu_custom_call" | custom-call | tf_op jit(solution)/shard_map/pallas_call | solution.py:172
  64.9 0.0 reduce-scatter.2.cloned.1.call-update
  64.9 0.0 all-gather.2.cloned.1.call-start
  65.0 43.8 %reduce-scatter.2.cloned.1.call-done.sum_ref = bf16[40,4864]{1,0:T(8,128)(2,1)} async-done(((bf16[320,4864]{1,0:T(8,128)(2,1)}), bf16[40,4864]{1,0:T(8,128)(2,1)}) %reduce-scatter.2.cloned.1.call-update) | async-done | bytes 389136 | tf_op jit(solution)/shard_map/reduce_scatter | solution.py:178
  108.8 1.0 copy-done.5
  109.8 1.1 shard_map.87
  110.9 0.0 all-gather.2.cloned.1.call-update
  110.9 53.1 %all-gather.2.cloned.1.call-done.join_ref = bf16[320,4992]{1,0:T(8,128)(2,1)} async-done(((bf16[40,4992]{1,0:T(8,128)(2,1)}), bf16[320,4992]{1,0:T(8,128)(2,1)}) %all-gather.2.cloned.1.call-update) | async-done | bytes 3194896 | tf_op jit(solution)/shard_map/all_gather | solution.py:184
  164.0 1.6 copy-done.3
  165.6 1.9 copy-done.4
  167.5 2.0 shard_map.88
  169.5 41.6 %all_to_all.11 = bf16[96,24,128]{2,1,0:T(8,128)(2,1)S(1)} all-to-all(bf16[96,24,128]{2,1,0:T(8,128)(2,1)S(1)} %bitcast.22), channel_id=1, replica_groups=mesh['dp'=96,'tensor'=8] {'dp'}, dimensions={0} | all-to-all | bytes 1179648 | tf_op jit(solution)/shard_map/all_to_all | solution.py:157
  211.1 0.0 copy-done.9
  211.1 1.3 shard_map.89
  (13 shorter events, 0.0 us)
Async XLA Ops:
  7.2 101.6 %reduce-scatter.2.cloned.1.call-start = ((), (), s32[]{:S(2)}) async-start(), calls=%async_computation.3 | async-start | bytes 3502080 | tf_op jit(solution)/shard_map/reduce_scatter | solution.py:178
  7.2 0.9 copy-start.6
  8.1 0.9 copy-start.7
  9.0 0.7 copy-start.8
  9.7 0.7 copy-start.10
  58.2 1.6 copy-start
  59.8 1.6 copy-start.2
  64.9 99.1 %copy-start.1 = (bf16[1,448,2432]{2,1,0:T(8,128)(2,1)S(1)}, bf16[1,448,2432]{2,1,0:T(8,128)(2,1)}, u32[]{:S(2)}) copy-start(bf16[1,448,2432]{2,1,0:T(8,128)(2,1)} %param.10) | copy-start | bytes 6537220
  64.9 99.0 %all-gather.2.cloned.1.call-start = ((), (), s32[]{:S(2)}) async-start(), calls=%async_computation.4 | async-start | bytes 3594240 | tf_op jit(solution)/shard_map/all_gather | solution.py:184
  108.8 1.0 copy-start.5
  164.0 1.6 copy-start.3
  165.6 1.9 copy-start.4
  167.5 43.6 %copy-start.9 = (s32[128,2]{0,1:T(2,128)S(1)}, s32[128,2]{0,1:T(2,128)}, u32[]{:S(2)}) copy-start(s32[128,2]{0,1:T(2,128)} %param.8) | copy-start | bytes 3076
  167.5 43.6 %copy-start.11 = (f32[128,2]{0,1:T(2,128)S(1)}, f32[128,2]{0,1:T(2,128)}, u32[]{:S(2)}) copy-start(f32[128,2]{0,1:T(2,128)} %param.9) | copy-start | bytes 3076
Sparse Core Ops, SparseCore 0:
  65.1 43.6 reduce-scatter.1
  111.1 52.7 all-gather.1

commit v2 on v1

--- a/solution.py
+++ b/solution.py
@@ -44,8 +44,45 @@
     return first, second
 
 
-def dispatch_kernel(ids_ref, probs_ref, tok_ref, cot_ref, out_ref, scratch):
+def chunks(size, step):
+    return [(at, min(at + step, size)) for at in range(0, size, step)]
+
+
+def copies(sources, targets, semaphores):
+    started = [
+        pltpu.make_async_copy(source, target, semaphores.at[i])
+        for i, (source, target) in enumerate(zip(sources, targets))
+    ]
+    for copy in started:
+        copy.start()
+    return started
+
+
+def dispatch_kernel(
+    ids_hbm,
+    probs_hbm,
+    tok_hbm,
+    cot_hbm,
+    up_hbm,
+    down_hbm,
+    out_ref,
+    up_ref,
+    down_ref,
+    scratch,
+    ids_ref,
+    probs_ref,
+    tok_ref,
+    cot_ref,
+    semaphores,
+):
     experts = out_ref.shape[0] // BLOCK
+    started = copies(
+        (ids_hbm, probs_hbm, tok_hbm, cot_hbm, up_hbm, down_hbm),
+        (ids_ref, probs_ref, tok_ref, cot_ref, up_ref, down_ref),
+        semaphores,
+    )
+    for copy in started[:4]:
+        copy.wait()
     named, slot = one_hots(ids_ref, experts)
     either = named[0] + named[1]
     weight = named[0] * probs_ref[0:1, :] + named[1] * probs_ref[1:2, :]
@@ -61,9 +98,11 @@
     for r in range(7 * CAP, BLOCK):
         scratch[pl.ds(r, experts, stride=BLOCK), :] = jnp.zeros((experts, LANES), F32)
     out_ref[...] = scratch[...].astype(BF16)
-
-
-def up_kernel(block_ref, up_ref, down_ref, out_ref, scratch):
+    for copy in started[4:]:
+        copy.wait()
+
+
+def up_kernel(block_ref, up_ref, down_ref, out_hbm, scratch, out_ref, semaphores):
     sources = block_ref.shape[0] // BLOCK
     hidden = up_ref.shape[1]
     scratch[...] = block_ref[...].astype(F32)
@@ -76,12 +115,21 @@
     pad = jnp.zeros((ROWS - CAP * sources, up_ref.shape[0]), F32)
     rows = jnp.concatenate(rows + [pad], axis=0).astype(BF16)
     grads = jnp.concatenate(grads + [pad], axis=0).astype(BF16)
+    started = []
     for left, weight, base in ((rows, up_ref, 0), (grads, down_ref, hidden)):
-        for at in range(0, hidden, 512):
-            to = min(at + 512, hidden)
-            out_ref[:, base + at : base + to] = jnp.dot(
+        for at, to in chunks(hidden, 512):
+            span = slice(base + at, base + to)
+            out_ref[:, span] = jnp.dot(
                 left, weight[:, at:to], preferred_element_type=F32
             ).astype(BF16)
+            started.append(
+                pltpu.make_async_copy(
+                    out_ref.at[:, span], out_hbm.at[:, span], semaphores.at[len(started)]
+                )
+            )
+            started[-1].start()
+    for copy in started:
+        copy.wait()
 
 
 def middle_kernel(sum_ref, out_ref):
@@ -102,17 +150,43 @@
     ).astype(BF16)
 
 
-def down_kernel(join_ref, up_ref, down_ref, out_ref, scratch):
+def columns_at(at, to):
+    return (slice(None), slice(at, to))
+
+
+def down_kernel(join_hbm, up_ref, down_hbm, out_ref, scratch, join_ref, down_ref, semaphores):
     sources = out_ref.shape[0] // BLOCK
     hidden = up_ref.shape[1]
     across = (((1,), (1,)), ((), ()))
-    out = lax.dot_general(
-        join_ref[:, :hidden], down_ref[...], across, preferred_element_type=F32
+    spans = chunks(hidden, 1024)
+    first = [columns_at(hidden + at, hidden + to) for at, to in spans]
+    second = [columns_at(at, to) for at, to in spans]
+    last = [columns_at(2 * hidden, 2 * hidden + LANES)]
+    own = [columns_at(at, to) for at, to in spans]
+    started = copies(
+        [join_hbm.at[part] for part in first]
+        + [down_hbm.at[part] for part in own]
+        + [join_hbm.at[part] for part in second + last],
+        [join_ref.at[part] for part in first]
+        + [down_ref.at[part] for part in own]
+        + [join_ref.at[part] for part in second + last],
+        semaphores,
     )
-    part = lax.dot_general(
-        join_ref[:, hidden : 2 * hidden], up_ref[...], across, preferred_element_type=F32
-    )
-    score = join_ref[:, 2 * hidden :].astype(F32)
+    count = len(spans)
+    part, out = 0.0, 0.0
+    for i in range(count):
+        started[i].wait()
+        part += lax.dot_general(
+            join_ref[first[i]], up_ref[own[i]], across, preferred_element_type=F32
+        )
+    for i in range(count):
+        started[count + i].wait()
+        started[2 * count + i].wait()
+        out += lax.dot_general(
+            join_ref[second[i]], down_ref[own[i]], across, preferred_element_type=F32
+        )
+    started[3 * count].wait()
+    score = join_ref[last[0]].astype(F32)
     for s in range(CAP):
         rows = slice(s * sources, (s + 1) * sources)
         for j in range(7):
@@ -152,6 +226,10 @@
     score_ref[...] = jnp.concatenate(scores, axis=0) / probs_ref[...]
 
 
+def in_hbm(array):
+    return pltpu.with_memory_space_constraint(array, pltpu.HBM)
+
+
 def exchange(block, experts):
     block = block.reshape(experts, BLOCK, LANES)
     block = lax.all_to_all(block, "dp", split_axis=0, concat_axis=0, tiled=True)
@@ -166,25 +244,56 @@
     up, down = up_weight[0], down_weight[0].T
     packed = jax.ShapeDtypeStruct((experts * BLOCK, LANES), BF16)
     stage = [pltpu.VMEM((experts * BLOCK, LANES), F32)]
-    send = pl.pallas_call(
-        dispatch_kernel, out_shape=packed, scratch_shapes=stage, compiler_params=params(16)
-    )(ids, probs, tokens.T, cotangent.T)
+    anywhere = pl.BlockSpec(memory_space=pltpu.HBM)
+    send, up_near, down_near = pl.pallas_call(
+        dispatch_kernel,
+        out_shape=(
+            packed,
+            pltpu.VMEM(up.shape, BF16),
+            pltpu.VMEM(down.shape, BF16),
+        ),
+        in_specs=[anywhere] * 6,
+        scratch_shapes=stage
+        + [
+            pltpu.VMEM(ids.shape, jnp.int32),
+            pltpu.VMEM(probs.shape, F32),
+            pltpu.VMEM((feat, count), BF16),
+            pltpu.VMEM((feat, count), BF16),
+            pltpu.SemaphoreType.DMA((6,)),
+        ],
+        compiler_params=params(14),
+    )(*map(in_hbm, (ids, probs, tokens.T, cotangent.T, up, down)))
     partial = pl.pallas_call(
         up_kernel,
         out_shape=jax.ShapeDtypeStruct((ROWS, 2 * hidden), BF16),
-        scratch_shapes=stage,
-        compiler_params=params(24),
-    )(exchange(send, experts), up, down)
+        out_specs=anywhere,
+        scratch_shapes=stage
+        + [
+            pltpu.VMEM((ROWS, 2 * hidden), BF16),
+            pltpu.SemaphoreType.DMA((2 * len(chunks(hidden, 512)),)),
+        ],
+        compiler_params=params(20),
+    )(exchange(send, experts), up_near, down_near)
     share = lax.psum_scatter(partial, "tensor", scatter_dimension=0, tiled=True)
     middle = pl.pallas_call(
         middle_kernel,
         out_shape=jax.ShapeDtypeStruct((share.shape[0], 2 * hidden + LANES), BF16),
-        compiler_params=params(16),
+        compiler_params=params(14),
     )(share)
     joined = lax.all_gather(middle, "tensor", axis=0, tiled=True)
+    whole = pl.BlockSpec(memory_space=pltpu.VMEM)
     back = pl.pallas_call(
-        down_kernel, out_shape=packed, scratch_shapes=stage, compiler_params=params(24)
-    )(joined, up, down)
+        down_kernel,
+        out_shape=packed,
+        in_specs=[anywhere, whole, anywhere],
+        scratch_shapes=stage
+        + [
+            pltpu.VMEM(joined.shape, BF16),
+            pltpu.VMEM(down.shape, BF16),
+            pltpu.SemaphoreType.DMA((3 * len(chunks(hidden, 1024)) + 1,)),
+        ],
+        compiler_params=params(20),
+    )(in_hbm(joined), up_near, in_hbm(down))
     mixed, input_grad, prob_grad = pl.pallas_call(
         combine_kernel,
         out_shape=(
@@ -193,7 +302,7 @@
             jax.ShapeDtypeStruct((2, count), F32),
         ),
         scratch_shapes=stage,
-        compiler_params=params(16),
+        compiler_params=params(14),
     )(ids, probs, exchange(back, experts))
     return mixed.T, input_grad.T, prob_grad.T
 

time: 220 us -> 214 us (0.973)
  local copies, waits for them, and re-layouts: 10.9 us -> 1.01 us
  Pallas kernels: 8.54 us -> 11.9 us
    unnamed x24 -> x6, local copies, waits for them, and re-layouts: 10.9 us -> 1.01 us
    pallas_call x2, Pallas kernels: 2.63 us -> 6.81 us  [the longest x1 4.32 us: per_device(): pl.pallas_call(down_kernel, out_shape=packed, in_specs=[anywhere, whole,...]
where the time goes in v2:
time: 214 us; the launch traced here: 213 us
  waiting for transfers between devices  97 us (45%)
  blocking collectives  88.7 us (41%)
  between operations  14.1 us (7%)
  Pallas kernels  11.9 us (6%)
    all_to_all x2, blocking collectives, exchange(): block = lax.all_to_all(block, 'dp', split_axis=0, concat_axis=0, tiled=True)  88.7 us
    all_gather x1, waiting for transfers between devices, per_device(): joined = lax.all_gather(middle, 'tensor', axis=0, tiled=True)  53.3 us
    reduce_scatter x1, waiting for transfers between devices, per_device(): share = lax.psum_scatter(partial, 'tensor', scatter_dimension=0, tiled=True)  43.7 us
    pallas_call x1, Pallas kernels, per_device(): pl.pallas_call(down_kernel, out_shape=packed, in_specs=[anywhere, whole,...  4.32 us
  transfers between devices with their start and end apart: 2, of which 2 were waited for; matrix products, arithmetic and copies ran while one was open for 0% of the time, Pallas kernels for 0%

profile of v2, /device:TPU:1, one launch (start us, length us, event | category | flops | bytes accessed | tf_op | source)
XLA Modules:
  0.0 212.8 jit_solution(17737141050087999368)
XLA Ops:
  7.2 0.0 reduce-scatter.2.cloned.1.call-start
  7.2 2.5 %shard_map.85 = (bf16[2304,128]{1,0:T(8,128)(2,1)S(1)}, bf16[448,2432]{1,0:T(8,128)(2,1)S(1)}, bf16[448,2432]{1,0:T(8,128)(2,1)S(1)}) custom-call(s32[2,128]{1,0:T(2,128)} %bitcast.19, f32[2,128]{1,0:T(2,128)} %bitcast.21, bf16[448,128]{1,0:T(8,128)(2,1)} %bitcast.26, bf16[448,128]{1,0:T(8,128)(2,1)} %bitcast.27, bf16[448,2432]{1,0:T(8,128)(2,1)} %bitcast.25, ...), custom_call_target="tpu_custom_call" | custom-call | tf_op jit(solution)/shard_map/pallas_call | solution.py:248
  9.7 47.1 %all_to_all.10 = bf16[96,24,128]{2,1,0:T(8,128)(2,1)S(1)} all-to-all(bf16[96,24,128]{2,1,0:T(8,128)(2,1)S(1)} %bitcast.18), channel_id=1, replica_groups=mesh['dp'=96,'tensor'=8] {'dp'}, dimensions={0} | all-to-all | bytes 1179648 | tf_op jit(solution)/shard_map/all_to_all | solution.py:235
  56.8 2.7 %shard_map.86 = bf16[320,4864]{1,0:T(8,128)(2,1)} custom-call(bf16[2304,128]{1,0:T(8,128)(2,1)S(1)} %bitcast.16, bf16[448,2432]{1,0:T(8,128)(2,1)S(1)} %get-tuple-element.10.up_ref, bf16[448,2432]{1,0:T(8,128)(2,1)S(1)} %get-tuple-element.11.down_ref), custom_call_target="tpu_custom_call" | custom-call | tf_op jit(solution)/shard_map/pallas_call | solution.py:266
  59.6 0.0 reduce-scatter.2.cloned.1.call-update
  59.6 0.0 all-gather.2.cloned.1.call-start
  59.7 43.7 %reduce-scatter.2.cloned.1.call-done.sum_ref = bf16[40,4864]{1,0:T(8,128)(2,1)} async-done(((bf16[320,4864]{1,0:T(8,128)(2,1)}), bf16[40,4864]{1,0:T(8,128)(2,1)}) %reduce-scatter.2.cloned.1.call-update) | async-done | bytes 389136 | tf_op jit(solution)/shard_map/reduce_scatter | solution.py:277
  103.3 0.0 copy-start
  103.3 1.0 copy-done
  104.3 1.1 shard_map.87
  105.4 0.0 all-gather.2.cloned.1.call-update
  105.4 0.0 copy-start.1
  105.4 0.0 copy-start.2
  105.4 53.3 %all-gather.2.cloned.1.call-done.join_hbm = bf16[320,4992]{1,0:T(8,128)(2,1)} async-done(((bf16[40,4992]{1,0:T(8,128)(2,1)}), bf16[320,4992]{1,0:T(8,128)(2,1)}) %all-gather.2.cloned.1.call-update) | async-done | bytes 3194896 | tf_op jit(solution)/shard_map/all_gather | solution.py:283
  158.7 4.3 %shard_map.88 = bf16[2304,128]{1,0:T(8,128)(2,1)S(1)} custom-call(bf16[320,4992]{1,0:T(8,128)(2,1)} %all-gather.2.cloned.1.call-done.join_hbm, bf16[448,2432]{1,0:T(8,128)(2,1)S(1)} %get-tuple-element.10.up_ref, bf16[448,2432]{1,0:T(8,128)(2,1)} %bitcast.24), custom_call_target="tpu_custom_call" | custom-call | tf_op jit(solution)/shard_map/pallas_call | solution.py:285
  163.1 41.6 %all_to_all.11 = bf16[96,24,128]{2,1,0:T(8,128)(2,1)S(1)} all-to-all(bf16[96,24,128]{2,1,0:T(8,128)(2,1)S(1)} %bitcast.17), channel_id=1, replica_groups=mesh['dp'=96,'tensor'=8] {'dp'}, dimensions={0} | all-to-all | bytes 1179648 | tf_op jit(solution)/shard_map/all_to_all | solution.py:235
  204.6 0.0 copy-done.1
  204.6 0.0 copy-done.2
  204.7 1.3 shard_map.89
Async XLA Ops:
  7.2 96.2 %reduce-scatter.2.cloned.1.call-start = ((), (), s32[]{:S(2)}) async-start(), calls=%async_computation.3 | async-start | bytes 3502080 | tf_op jit(solution)/shard_map/reduce_scatter | solution.py:277
  59.6 99.1 %all-gather.2.cloned.1.call-start = ((), (), s32[]{:S(2)}) async-start(), calls=%async_computation.4 | async-start | bytes 3594240 | tf_op jit(solution)/shard_map/all_gather | solution.py:283
  103.3 1.0 copy-start
  105.4 99.2 %copy-start.1 = (s32[128,2]{0,1:T(2,128)S(1)}, s32[128,2]{0,1:T(2,128)}, u32[]{:S(2)}) copy-start(s32[128,2]{0,1:T(2,128)} %param.8) | copy-start | bytes 3076
  105.4 99.2 %copy-start.2 = (f32[128,2]{0,1:T(2,128)S(1)}, f32[128,2]{0,1:T(2,128)}, u32[]{:S(2)}) copy-start(f32[128,2]{0,1:T(2,128)} %param.9) | copy-start | bytes 3076
Sparse Core Ops, SparseCore 0:
  59.7 43.5 reduce-scatter.1
  105.7 52.9 all-gather.1

commit v3 on v2

--- a/solution.py
+++ b/solution.py
@@ -1,3 +1,5 @@
+import functools
+
 import jax
 import jax.numpy as jnp
 from jax import lax
@@ -8,7 +10,10 @@
 CAP = 3
 LANES = 128
 BLOCK = 24
-ROWS = 320
+SHARE = 40
+HEAD = 16
+SMALL = 8
+LARGE = 16
 F32 = jnp.float32
 BF16 = jnp.bfloat16
 MIB = 1024 * 1024
@@ -102,19 +107,34 @@
         copy.wait()
 
 
-def up_kernel(block_ref, up_ref, down_ref, out_hbm, scratch, out_ref, semaphores):
+def row_of(device, slot, each):
+    return device * SHARE + (HEAD + (slot - 1) * each if slot else 0)
+
+
+def up_kernel(
+    block_ref, up_ref, down_ref, out_hbm, scratch, row_ref, grad_ref, out_ref, semaphores
+):
     sources = block_ref.shape[0] // BLOCK
-    hidden = up_ref.shape[1]
+    feat, hidden = up_ref.shape
+    devices = out_ref.shape[0] // SHARE
+    each = sources // devices
     scratch[...] = block_ref[...].astype(F32)
-    rows, grads = [], []
-    for s in range(CAP):
-        tiles = [scratch[pl.ds(s * 7 + j, sources, stride=BLOCK), :] for j in range(7)]
-        first, second = pair_of(tiles)
-        rows.append(first)
-        grads.append(second)
-    pad = jnp.zeros((ROWS - CAP * sources, up_ref.shape[0]), F32)
-    rows = jnp.concatenate(rows + [pad], axis=0).astype(BF16)
-    grads = jnp.concatenate(grads + [pad], axis=0).astype(BF16)
+    for d in range(devices):
+        for s in range(CAP):
+            rows = slice(row_of(d, s, each), row_of(d, s, each) + each)
+            for j in range(7):
+                tile = scratch[pl.ds(d * each * BLOCK + s * 7 + j, each, stride=BLOCK), :]
+                if j < 3:
+                    row_ref[rows, j * LANES : (j + 1) * LANES] = tile
+                elif j < 6:
+                    grad_ref[rows, (j - 3) * LANES : (j - 2) * LANES] = tile
+                else:
+                    row_ref[rows, 3 * LANES :] = tile
+        pad = slice(d * SHARE + each, d * SHARE + HEAD)
+        row_ref[pad, :] = jnp.zeros((HEAD - each, row_ref.shape[1]), F32)
+        grad_ref[pad, :] = jnp.zeros((HEAD - each, grad_ref.shape[1]), F32)
+    rows = row_ref[:, :feat].astype(BF16)
+    grads = jnp.concatenate([grad_ref[...], row_ref[:, feat:]], axis=1).astype(BF16)
     started = []
     for left, weight, base in ((rows, up_ref, 0), (grads, down_ref, hidden)):
         for at, to in chunks(hidden, 512):
@@ -132,84 +152,175 @@
         copy.wait()
 
 
-def middle_kernel(sum_ref, out_ref):
+def middle_kernel(sum_ref, small_ref, large_ref, scratch):
     hidden = sum_ref.shape[1] // 2
+    each = small_ref.shape[0] // 2
     up_sum = sum_ref[:, :hidden].astype(F32)
     grad = sum_ref[:, hidden:].astype(F32)
     sigmoid = 1.0 / (1.0 + jnp.exp(-up_sum))
-    act = (up_sum * sigmoid).astype(BF16)
-    out_ref[:, :hidden] = act
-    out_ref[:, hidden : 2 * hidden] = (
-        grad * sigmoid * (1.0 + up_sum * (1.0 - sigmoid))
-    ).astype(BF16)
-    score = jnp.sum(act.astype(F32) * grad, axis=1, keepdims=True)
+    act = (up_sum * sigmoid).astype(BF16).astype(F32)
+    up_grad = grad * sigmoid * (1.0 + up_sum * (1.0 - sigmoid))
+    score = jnp.sum(act * grad, axis=1, keepdims=True)
     high = score.astype(BF16).astype(F32)
     lane = lax.broadcasted_iota(jnp.int32, (sum_ref.shape[0], LANES), 1)
-    out_ref[:, 2 * hidden :] = jnp.where(
-        lane == 0, high, jnp.where(lane == 1, score - high, 0.0)
-    ).astype(BF16)
+    score = jnp.where(lane == 0, high, jnp.where(lane == 1, score - high, 0.0))
+    scratch[:each, :hidden] = act[:each]
+    scratch[each:, :hidden] = up_grad[:each]
+    scratch[:each, hidden:] = score[:each]
+    scratch[each:, hidden:] = jnp.zeros((each, LANES), F32)
+    small_ref[...] = scratch[...].astype(BF16)
+    rest = slice(HEAD, HEAD + 2 * each)
+    large_ref[:, :hidden] = act[rest].astype(BF16)
+    large_ref[:, hidden : 2 * hidden] = up_grad[rest].astype(BF16)
+    large_ref[:, 2 * hidden :] = score[rest].astype(BF16)
 
 
 def columns_at(at, to):
     return (slice(None), slice(at, to))
 
 
-def down_kernel(join_hbm, up_ref, down_hbm, out_ref, scratch, join_ref, down_ref, semaphores):
-    sources = out_ref.shape[0] // BLOCK
+def pack(out_ref, part_ref, scores, target, rows, devices, each, slots, height):
+    for d in range(devices):
+        for s in range(slots):
+            low, high = rows(d, s)
+            left = slice(low, low + each)
+            right = slice(high, high + each)
+            out, part = out_ref[left, :], part_ref[right, :]
+            for j in range(7):
+                target[pl.ds(d * each * height + s * 7 + j, each, stride=height), :] = tile_of(
+                    out, part, j
+                )
+            target[pl.ds(d * each * height + 7 * slots + s, each, stride=height), :] = scores[
+                left, :
+            ]
+
+
+def down_small_kernel(
+    devices,
+    join_hbm,
+    up_ref,
+    down_hbm,
+    out_ref,
+    target,
+    join_ref,
+    down_ref,
+    out_rows,
+    part_rows,
+    score_rows,
+    semaphores,
+):
+    hidden = up_ref.shape[1]
+    across = (((1,), (1,)), ((), ()))
+    started = copies((join_hbm, down_hbm), (join_ref, down_ref), semaphores)
+    started[0].wait()
+    joined = join_ref[:, :hidden]
+    part_rows[...] = lax.dot_general(joined, up_ref[...], across, preferred_element_type=F32)
+    score_rows[...] = join_ref[:, hidden:].astype(F32)
+    started[1].wait()
+    out_rows[...] = lax.dot_general(joined, down_ref[...], across, preferred_element_type=F32)
+    each = join_ref.shape[0] // devices // 2
+    pack(
+        out_rows,
+        part_rows,
+        score_rows,
+        target,
+        lambda d, s: (2 * each * d, 2 * each * d + each),
+        devices,
+        each,
+        1,
+        SMALL,
+    )
+    out_ref[...] = target[...].astype(BF16)
+
+
+def down_large_kernel(
+    devices,
+    join_hbm,
+    up_ref,
+    down_hbm,
+    out_ref,
+    target,
+    join_ref,
+    down_ref,
+    out_rows,
+    part_rows,
+    score_rows,
+    semaphores,
+):
     hidden = up_ref.shape[1]
     across = (((1,), (1,)), ((), ()))
     spans = chunks(hidden, 1024)
-    first = [columns_at(hidden + at, hidden + to) for at, to in spans]
-    second = [columns_at(at, to) for at, to in spans]
-    last = [columns_at(2 * hidden, 2 * hidden + LANES)]
+    parts = [columns_at(base + at, base + to) for base in (hidden, 0) for at, to in spans]
+    parts.append(columns_at(2 * hidden, 2 * hidden + LANES))
     own = [columns_at(at, to) for at, to in spans]
+    count = len(spans)
+    from_join = copies(
+        [join_hbm.at[part] for part in parts[:count]],
+        [join_ref.at[part] for part in parts[:count]],
+        semaphores,
+    )
+    from_down = copies(
+        [down_hbm.at[part] for part in own],
+        [down_ref.at[part] for part in own],
+        semaphores.at[pl.ds(count, count)],
+    )
     started = copies(
-        [join_hbm.at[part] for part in first]
-        + [down_hbm.at[part] for part in own]
-        + [join_hbm.at[part] for part in second + last],
-        [join_ref.at[part] for part in first]
-        + [down_ref.at[part] for part in own]
-        + [join_ref.at[part] for part in second + last],
-        semaphores,
-    )
-    count = len(spans)
-    part, out = 0.0, 0.0
+        [join_hbm.at[part] for part in parts[count:]],
+        [join_ref.at[part] for part in parts[count:]],
+        semaphores.at[pl.ds(2 * count, count + 1)],
+    )
+    total = 0.0
     for i in range(count):
+        from_join[i].wait()
+        total += lax.dot_general(
+            join_ref[parts[i]], up_ref[own[i]], across, preferred_element_type=F32
+        )
+    part_rows[...] = total
+    total = 0.0
+    for i in range(count):
+        from_down[i].wait()
         started[i].wait()
-        part += lax.dot_general(
-            join_ref[first[i]], up_ref[own[i]], across, preferred_element_type=F32
+        total += lax.dot_general(
+            join_ref[parts[count + i]], down_ref[own[i]], across, preferred_element_type=F32
         )
-    for i in range(count):
-        started[count + i].wait()
-        started[2 * count + i].wait()
-        out += lax.dot_general(
-            join_ref[second[i]], down_ref[own[i]], across, preferred_element_type=F32
-        )
-    started[3 * count].wait()
-    score = join_ref[last[0]].astype(F32)
-    for s in range(CAP):
-        rows = slice(s * sources, (s + 1) * sources)
-        for j in range(7):
-            scratch[pl.ds(s * 7 + j, sources, stride=BLOCK), :] = tile_of(out[rows], part[rows], j)
-        scratch[pl.ds(7 * CAP + s, sources, stride=BLOCK), :] = score[rows]
-    out_ref[...] = scratch[...].astype(BF16)
-
-
-def combine_kernel(ids_ref, probs_ref, block_ref, mixed_ref, grad_ref, score_ref, scratch):
-    experts = block_ref.shape[0] // BLOCK
+    out_rows[...] = total
+    started[-1].wait()
+    score_rows[...] = join_ref[parts[-1]].astype(F32)
+    each = join_ref.shape[0] // devices // 2
+
+    def rows(d, s):
+        return ((2 * d + s) * each,) * 2
+
+    pack(
+        out_rows, part_rows, score_rows, target, rows, devices, each, 2, LARGE
+    )
+    out_ref[...] = target[...].astype(BF16)
+
+
+def combine_kernel(
+    ids_ref, probs_ref, small_ref, large_ref, mixed_ref, grad_ref, score_ref, first_rows, rest_rows
+):
+    experts = small_ref.shape[0] // SMALL
     named, slot = one_hots(ids_ref, experts)
-    scratch[...] = block_ref[...].astype(F32)
+    first_rows[...] = small_ref[...].astype(F32)
+    rest_rows[...] = large_ref[...].astype(F32)
+
+    def came(slot, j):
+        if slot == 0:
+            return first_rows[pl.ds(j, experts, stride=SMALL), :]
+        at = (slot - 1) * 7 + j if j < 7 else 14 + slot - 1
+        return rest_rows[pl.ds(at, experts, stride=LARGE), :]
+
     along = (((0,), (0,)), ((), ()))
     outs, parts, picks = [], [], []
     scores = [jnp.zeros((1, ids_ref.shape[1]), F32) for _ in range(2)]
     for s in range(CAP):
         here = (slot == s).astype(F32)
-        tiles = [scratch[pl.ds(s * 7 + j, experts, stride=BLOCK), :] for j in range(7)]
-        first, second = pair_of(tiles)
+        first, second = pair_of([came(s, j) for j in range(7)])
         outs.append(first)
         parts.append(second)
         picks.append(jnp.concatenate([named[0] * here, named[1] * here], axis=1))
-        tail = scratch[pl.ds(7 * CAP + s, experts, stride=BLOCK), :]
+        tail = came(s, 7)
         value = tail[:, 0:1] + tail[:, 1:2]
         for k in range(2):
             scores[k] += jnp.sum(named[k] * here * value, axis=0, keepdims=True)
@@ -231,9 +342,10 @@
 
 
 def exchange(block, experts):
-    block = block.reshape(experts, BLOCK, LANES)
+    shape = block.shape
+    block = block.reshape(experts, -1, LANES)
     block = lax.all_to_all(block, "dp", split_axis=0, concat_axis=0, tiled=True)
-    return block.reshape(experts * BLOCK, LANES)
+    return block.reshape(shape)
 
 
 def per_device(tokens, cotangent, expert_ids, route_probs, up_weight, down_weight):
@@ -263,35 +375,64 @@
         ],
         compiler_params=params(14),
     )(*map(in_hbm, (ids, probs, tokens.T, cotangent.T, up, down)))
+    devices = lax.axis_size("tensor")
+    each = experts // devices
     partial = pl.pallas_call(
         up_kernel,
-        out_shape=jax.ShapeDtypeStruct((ROWS, 2 * hidden), BF16),
+        out_shape=pltpu.HBM((devices * SHARE, 2 * hidden), BF16),
         out_specs=anywhere,
         scratch_shapes=stage
         + [
-            pltpu.VMEM((ROWS, 2 * hidden), BF16),
+            pltpu.VMEM((devices * SHARE, 4 * LANES), F32),
+            pltpu.VMEM((devices * SHARE, 3 * LANES), F32),
+            pltpu.VMEM((devices * SHARE, 2 * hidden), BF16),
             pltpu.SemaphoreType.DMA((2 * len(chunks(hidden, 512)),)),
         ],
         compiler_params=params(20),
     )(exchange(send, experts), up_near, down_near)
     share = lax.psum_scatter(partial, "tensor", scatter_dimension=0, tiled=True)
-    middle = pl.pallas_call(
+    small, large = pl.pallas_call(
         middle_kernel,
-        out_shape=jax.ShapeDtypeStruct((share.shape[0], 2 * hidden + LANES), BF16),
+        out_shape=(
+            jax.ShapeDtypeStruct((2 * each, hidden + LANES), BF16),
+            jax.ShapeDtypeStruct((2 * each, 2 * hidden + LANES), BF16),
+        ),
+        scratch_shapes=[pltpu.VMEM((2 * each, hidden + LANES), F32)],
         compiler_params=params(14),
     )(share)
-    joined = lax.all_gather(middle, "tensor", axis=0, tiled=True)
     whole = pl.BlockSpec(memory_space=pltpu.VMEM)
+    joined = lax.all_gather(large, "tensor", axis=0, tiled=True)
+    joined_small = lax.all_gather(small, "tensor", axis=0, tiled=True)
+    products = [
+        pltpu.VMEM((2 * each * devices, feat), F32),
+        pltpu.VMEM((2 * each * devices, feat), F32),
+        pltpu.VMEM((2 * each * devices, LANES), F32),
+    ]
+    back_small = pl.pallas_call(
+        functools.partial(down_small_kernel, devices),
+        out_shape=jax.ShapeDtypeStruct((experts * SMALL, LANES), BF16),
+        in_specs=[anywhere, whole, anywhere],
+        scratch_shapes=[
+            pltpu.VMEM((experts * SMALL, LANES), F32),
+            pltpu.VMEM(joined_small.shape, BF16),
+            pltpu.VMEM(down.shape, BF16),
+        ]
+        + products
+        + [pltpu.SemaphoreType.DMA((2,))],
+        compiler_params=params(20),
+    )(in_hbm(joined_small), up_near, in_hbm(down))
+    back_small = exchange(back_small, experts)
     back = pl.pallas_call(
-        down_kernel,
-        out_shape=packed,
+        functools.partial(down_large_kernel, devices),
+        out_shape=jax.ShapeDtypeStruct((experts * LARGE, LANES), BF16),
         in_specs=[anywhere, whole, anywhere],
-        scratch_shapes=stage
-        + [
+        scratch_shapes=[
+            pltpu.VMEM((experts * LARGE, LANES), F32),
             pltpu.VMEM(joined.shape, BF16),
             pltpu.VMEM(down.shape, BF16),
-            pltpu.SemaphoreType.DMA((3 * len(chunks(hidden, 1024)) + 1,)),
-        ],
+        ]
+        + products
+        + [pltpu.SemaphoreType.DMA((3 * len(chunks(hidden, 1024)) + 1,))],
         compiler_params=params(20),
     )(in_hbm(joined), up_near, in_hbm(down))
     mixed, input_grad, prob_grad = pl.pallas_call(
@@ -301,9 +442,12 @@
             jax.ShapeDtypeStruct((feat, count), BF16),
             jax.ShapeDtypeStruct((2, count), F32),
         ),
-        scratch_shapes=stage,
+        scratch_shapes=[
+            pltpu.VMEM((experts * SMALL, LANES), F32),
+            pltpu.VMEM((experts * LARGE, LANES), F32),
+        ],
         compiler_params=params(14),
-    )(ids, probs, exchange(back, experts))
+    )(ids, probs, back_small, exchange(back, experts))
     return mixed.T, input_grad.T, prob_grad.T
 
 

time: 214 us -> 209 us (0.977)
  waiting for transfers between devices: 97 us -> 56.3 us
  starting transfers between devices: 0.08 us -> 23.6 us
  blocking collectives: 88.7 us -> 98.1 us
  Pallas kernels: 11.9 us -> 14.7 us
    all_gather x1, waiting for transfers between devices: 53.3 us -> 0.02 us  [per_device(): joined = lax.all_gather(large, 'tensor', axis=0, tiled=True)]
    all_to_all x0 -> x1, starting transfers between devices: none -> 23.5 us  [exchange(): block = lax.all_to_all(block, 'dp', split_axis=0, concat_axis=0, tiled=True)]
    all_gather x0 -> x1, blocking collectives: none -> 22.9 us  [per_device(): joined_small = lax.all_gather(small, 'tensor', axis=0, tiled=True)]
    all_to_all x2, blocking collectives: 88.7 us -> 75.3 us  [exchange(): block = lax.all_to_all(block, 'dp', split_axis=0, concat_axis=0, tiled=True)]
    all_to_all x0 -> x1, waiting for transfers between devices: none -> 12.5 us  [exchange(): block = lax.all_to_all(block, 'dp', split_axis=0, concat_axis=0, tiled=True)]
    pallas_call x3 -> x4, Pallas kernels: 8.13 us -> 10.9 us  [the longest x1 3.64 us: per_device(): pl.pallas_call(functools.partial(down_small_kernel, devices), out_shape=j...]
  transfers between devices with their start and end apart: 2 -> 3, of which waited for: 2 -> 2; matrix products, arithmetic and copies ran while one was open for 0% -> 0% of each run, Pallas kernels for 0% -> 3%
where the time goes in v3:
time: 209 us; the launch traced here: 208 us
  blocking collectives  98.1 us (47%)
  waiting for transfers between devices  56.3 us (27%)
  starting transfers between devices  23.6 us (11%)
  Pallas kernels  14.7 us (7%)
  between operations  14.1 us (7%)
    all_to_all x2, blocking collectives, exchange(): block = lax.all_to_all(block, 'dp', split_axis=0, concat_axis=0, tiled=True)  75.3 us
    reduce_scatter x1, waiting for transfers between devices, per_device(): share = lax.psum_scatter(partial, 'tensor', scatter_dimension=0, tiled=True)  43.7 us
    all_to_all x1, starting transfers between devices, exchange(): block = lax.all_to_all(block, 'dp', split_axis=0, concat_axis=0, tiled=True)  23.5 us
    all_gather x1, blocking collectives, per_device(): joined_small = lax.all_gather(small, 'tensor', axis=0, tiled=True)  22.9 us
    all_to_all x1, waiting for transfers between devices, exchange(): block = lax.all_to_all(block, 'dp', split_axis=0, concat_axis=0, tiled=True)  12.5 us
  transfers between devices with their start and end apart: 3, of which 2 were waited for; matrix products, arithmetic and copies ran while one was open for 0% of the time, Pallas kernels for 3%

profile of v3, /device:TPU:1, one launch (start us, length us, event | category | flops | bytes accessed | tf_op | source)
XLA Modules:
  0.0 207.8 jit_solution(8882823271083656317)
XLA Ops:
  7.2 0.0 reduce-scatter.2.cloned.1.call-start
  7.2 2.5 %shard_map.85 = (bf16[2304,128]{1,0:T(8,128)(2,1)S(1)}, bf16[448,2432]{1,0:T(8,128)(2,1)S(1)}, bf16[448,2432]{1,0:T(8,128)(2,1)S(1)}) custom-call(s32[2,128]{1,0:T(2,128)} %bitcast.22, f32[2,128]{1,0:T(2,128)} %bitcast.24, bf16[448,128]{1,0:T(8,128)(2,1)} %bitcast.30, bf16[448,128]{1,0:T(8,128)(2,1)} %bitcast.31, bf16[448,2432]{1,0:T(8,128)(2,1)} %bitcast.29, ...), custom_call_target="tpu_custom_call" | custom-call | tf_op jit(solution)/shard_map/pallas_call | solution.py:360
  9.7 47.1 %all_to_all.15 = bf16[96,24,128]{2,1,0:T(8,128)(2,1)S(1)} all-to-all(bf16[96,24,128]{2,1,0:T(8,128)(2,1)S(1)} %bitcast.21), channel_id=1, replica_groups=mesh['dp'=96,'tensor'=8] {'dp'}, dimensions={0} | all-to-all | bytes 1179648 | tf_op jit(solution)/shard_map/all_to_all | solution.py:347
  56.8 2.7 %shard_map.86 = bf16[320,4864]{1,0:T(8,128)(2,1)} custom-call(bf16[2304,128]{1,0:T(8,128)(2,1)S(1)} %bitcast.17, bf16[448,2432]{1,0:T(8,128)(2,1)S(1)} %get-tuple-element.12.up_ref, bf16[448,2432]{1,0:T(8,128)(2,1)S(1)} %get-tuple-element.13.down_ref), custom_call_target="tpu_custom_call" | custom-call | tf_op jit(solution)/shard_map/pallas_call | solution.py:380
  59.6 0.0 reduce-scatter.2.cloned.1.call-update
  59.6 0.0 all-gather.2.cloned.1.call-start
  59.7 43.7 %reduce-scatter.2.cloned.1.call-done.sum_ref = bf16[40,4864]{1,0:T(8,128)(2,1)} async-done(((bf16[320,4864]{1,0:T(8,128)(2,1)}), bf16[40,4864]{1,0:T(8,128)(2,1)}) %reduce-scatter.2.cloned.1.call-update) | async-done | bytes 389136 | tf_op jit(solution)/shard_map/reduce_scatter | solution.py:393
  103.4 0.0 copy-start
  103.4 1.0 copy-done
  104.4 1.1 shard_map.87
  105.5 0.0 all-gather.2.cloned.1.call-update
  105.5 22.9 %all_gather.6.join_hbm = bf16[192,2560]{1,0:T(8,128)(2,1)} all-gather(bf16[24,2560]{1,0:T(8,128)(2,1)S(1)} %get-tuple-element.14), channel_id=1, replica_groups=mesh['dp'=96,'tensor'=8] {'tensor'}, dimensions={0}, use_global_device_ids=true | all-gather | bytes 1105920 | tf_op jit(solution)/shard_map/all_gather | solution.py:405
  128.4 3.6 %shard_map.88 = bf16[768,128]{1,0:T(8,128)(2,1)} custom-call(bf16[192,2560]{1,0:T(8,128)(2,1)} %all_gather.6.join_hbm, bf16[448,2432]{1,0:T(8,128)(2,1)S(1)} %get-tuple-element.12.up_ref, bf16[448,2432]{1,0:T(8,128)(2,1)} %bitcast.27), custom_call_target="tpu_custom_call" | custom-call | tf_op jit(solution)/shard_map/pallas_call | solution.py:411
  132.0 23.5 %all-to-all-start.1 = ((bf16[96,8,128]{2,1,0:T(8,128)(2,1)}), bf16[96,8,128]{2,1,0:T(8,128)(2,1)S(1)}, u32[]{:S(2)}, u32[]{:S(2)}) async-start(bf16[96,8,128]{2,1,0:T(8,128)(2,1)} %bitcast.9), calls=%async_computation.2 | async-start | bytes 393216 | tf_op jit(solution)/shard_map/all_to_all | solution.py:347
  155.5 0.0 copy-start.1
  155.5 0.0 copy-start.2
  155.6 0.0 all-gather.2.cloned.1.call-done.join_hbm
  155.6 3.4 %shard_map.89 = bf16[1536,128]{1,0:T(8,128)(2,1)S(1)} custom-call(bf16[192,4992]{1,0:T(8,128)(2,1)} %all-gather.2.cloned.1.call-done.join_hbm, bf16[448,2432]{1,0:T(8,128)(2,1)S(1)} %get-tuple-element.12.up_ref, bf16[448,2432]{1,0:T(8,128)(2,1)} %bitcast.28), custom_call_target="tpu_custom_call" | custom-call | tf_op jit(solution)/shard_map/pallas_call | solution.py:425
  159.0 12.5 %all-to-all-done.1 = bf16[96,8,128]{2,1,0:T(8,128)(2,1)S(1)} async-done(((bf16[96,8,128]{2,1,0:T(8,128)(2,1)}), bf16[96,8,128]{2,1,0:T(8,128)(2,1)S(1)}, u32[]{:S(2)}, u32[]{:S(2)}) %all-to-all-start.1) | async-done | bytes 196640 | tf_op jit(solution)/shard_map/all_to_all | solution.py:347
  171.5 28.1 %all_to_all.16 = bf16[96,16,128]{2,1,0:T(8,128)(2,1)S(1)} all-to-all(bf16[96,16,128]{2,1,0:T(8,128)(2,1)S(1)} %bitcast.18), channel_id=1, replica_groups=mesh['dp'=96,'tensor'=8] {'dp'}, dimensions={0} | all-to-all | bytes 786432 | tf_op jit(solution)/shard_map/all_to_all | solution.py:347
  199.6 0.0 copy-done.1
  199.6 0.0 copy-done.2
  199.6 1.3 shard_map.90
Async XLA Ops:
  7.2 96.2 %reduce-scatter.2.cloned.1.call-start = ((), (), s32[]{:S(2)}) async-start(), calls=%async_computation.4 | async-start | bytes 3502080 | tf_op jit(solution)/shard_map/reduce_scatter | solution.py:393
  59.6 96.0 %all-gather.2.cloned.1.call-start = ((), (), s32[]{:S(2)}) async-start(), calls=%async_computation.5 | async-start | bytes 2156544 | tf_op jit(solution)/shard_map/all_gather | solution.py:404
  103.4 1.0 copy-start
  132.0 39.5 %all-to-all-start.1 = ((bf16[96,8,128]{2,1,0:T(8,128)(2,1)}), bf16[96,8,128]{2,1,0:T(8,128)(2,1)S(1)}, u32[]{:S(2)}, u32[]{:S(2)}) async-start(bf16[96,8,128]{2,1,0:T(8,128)(2,1)} %bitcast.9), calls=%async_computation.2 | async-start | bytes 393216 | tf_op jit(solution)/shard_map/all_to_all | solution.py:347
  155.5 44.1 %copy-start.1 = (s32[128,2]{0,1:T(2,128)S(1)}, s32[128,2]{0,1:T(2,128)}, u32[]{:S(2)}) copy-start(s32[128,2]{0,1:T(2,128)} %param.8) | copy-start | bytes 3076
  155.5 44.1 %copy-start.2 = (f32[128,2]{0,1:T(2,128)S(1)}, f32[128,2]{0,1:T(2,128)}, u32[]{:S(2)}) copy-start(f32[128,2]{0,1:T(2,128)} %param.9) | copy-start | bytes 3076
Sparse Core Ops, SparseCore 0:
  59.7 43.6 reduce-scatter.1
  105.8 45.8 all-gather.1

commit v4 on v3

--- a/solution.py
+++ b/solution.py
@@ -238,6 +238,7 @@
     join_hbm,
     up_ref,
     down_hbm,
+    _,
     out_ref,
     target,
     join_ref,
@@ -425,7 +426,7 @@
     back = pl.pallas_call(
         functools.partial(down_large_kernel, devices),
         out_shape=jax.ShapeDtypeStruct((experts * LARGE, LANES), BF16),
-        in_specs=[anywhere, whole, anywhere],
+        in_specs=[anywhere, whole, anywhere, pl.BlockSpec(memory_space=pl.ANY)],
         scratch_shapes=[
             pltpu.VMEM((experts * LARGE, LANES), F32),
             pltpu.VMEM(joined.shape, BF16),
@@ -434,7 +435,7 @@
         + products
         + [pltpu.SemaphoreType.DMA((3 * len(chunks(hidden, 1024)) + 1,))],
         compiler_params=params(20),
-    )(in_hbm(joined), up_near, in_hbm(down))
+    )(in_hbm(joined), up_near, in_hbm(down), back_small)
     mixed, input_grad, prob_grad = pl.pallas_call(
         combine_kernel,
         out_shape=(

time: 209 us -> 211 us (level)
  blocking collectives: 98.1 us -> 137 us
  starting transfers between devices: 23.6 us -> 0.08 us
  waiting for transfers between devices: 56.3 us -> 43.8 us
    all_to_all x2 -> x3, blocking collectives: 75.3 us -> 115 us  [exchange(): block = lax.all_to_all(block, 'dp', split_axis=0, concat_axis=0, tiled=True)]
    all_to_all x1 -> x0, starting transfers between devices: 23.5 us -> none  [exchange(): block = lax.all_to_all(block, 'dp', split_axis=0, concat_axis=0, tiled=True)]
    all_to_all x1 -> x0, waiting for transfers between devices: 12.5 us -> none  [exchange(): block = lax.all_to_all(block, 'dp', split_axis=0, concat_axis=0, tiled=True)]
  transfers between devices with their start and end apart: 3 -> 2, of which waited for: 2 -> 1; matrix products, arithmetic and copies ran while one was open for 0% -> 0% of each run, Pallas kernels for 3% -> 1%
where the time goes in v4:
time: 211 us; the launch traced here: 210 us
  blocking collectives  137 us (65%)
  waiting for transfers between devices  43.8 us (21%)
  between operations  14.1 us (7%)
  Pallas kernels  14 us (7%)
    all_to_all x3, blocking collectives, exchange(): block = lax.all_to_all(block, 'dp', split_axis=0, concat_axis=0, tiled=True)  115 us
    reduce_scatter x1, waiting for transfers between devices, per_device(): share = lax.psum_scatter(partial, 'tensor', scatter_dimension=0, tiled=True)  43.7 us
    all_gather x1, blocking collectives, per_device(): joined_small = lax.all_gather(small, 'tensor', axis=0, tiled=True)  22.9 us
  transfers between devices with their start and end apart: 2, of which 1 were waited for; matrix products, arithmetic and copies ran while one was open for 0% of the time, Pallas kernels for 1%

profile of v4, /device:TPU:1, one launch (start us, length us, event | category | flops | bytes accessed | tf_op | source)
XLA Modules:
  0.0 210.4 jit_solution(2760426623397737764)
XLA Ops:
  7.2 0.0 reduce-scatter.2.cloned.1.call-start
  7.2 2.5 %shard_map.85 = (bf16[2304,128]{1,0:T(8,128)(2,1)S(1)}, bf16[448,2432]{1,0:T(8,128)(2,1)S(1)}, bf16[448,2432]{1,0:T(8,128)(2,1)S(1)}) custom-call(s32[2,128]{1,0:T(2,128)} %bitcast.24, f32[2,128]{1,0:T(2,128)} %bitcast.26, bf16[448,128]{1,0:T(8,128)(2,1)} %bitcast.32, bf16[448,128]{1,0:T(8,128)(2,1)} %bitcast.33, bf16[448,2432]{1,0:T(8,128)(2,1)} %bitcast.31, ...), custom_call_target="tpu_custom_call" | custom-call | tf_op jit(solution)/shard_map/pallas_call | solution.py:361
  9.7 47.1 %all_to_all.15 = bf16[96,24,128]{2,1,0:T(8,128)(2,1)S(1)} all-to-all(bf16[96,24,128]{2,1,0:T(8,128)(2,1)S(1)} %bitcast.23), channel_id=1, replica_groups=mesh['dp'=96,'tensor'=8] {'dp'}, dimensions={0} | all-to-all | bytes 1179648 | tf_op jit(solution)/shard_map/all_to_all | solution.py:348
  56.8 2.7 %shard_map.86 = bf16[320,4864]{1,0:T(8,128)(2,1)} custom-call(bf16[2304,128]{1,0:T(8,128)(2,1)S(1)} %bitcast.17, bf16[448,2432]{1,0:T(8,128)(2,1)S(1)} %get-tuple-element.12.up_ref, bf16[448,2432]{1,0:T(8,128)(2,1)S(1)} %get-tuple-element.13.down_ref), custom_call_target="tpu_custom_call" | custom-call | tf_op jit(solution)/shard_map/pallas_call | solution.py:381
  59.6 0.0 reduce-scatter.2.cloned.1.call-update
  59.6 0.0 all-gather.2.cloned.1.call-start
  59.7 43.7 %reduce-scatter.2.cloned.1.call-done.sum_ref = bf16[40,4864]{1,0:T(8,128)(2,1)} async-done(((bf16[320,4864]{1,0:T(8,128)(2,1)}), bf16[40,4864]{1,0:T(8,128)(2,1)}) %reduce-scatter.2.cloned.1.call-update) | async-done | bytes 389136 | tf_op jit(solution)/shard_map/reduce_scatter | solution.py:394
  103.4 0.0 copy-start
  103.4 1.0 copy-done
  104.4 1.0 shard_map.87
  105.4 0.0 all-gather.2.cloned.1.call-update
  105.5 22.9 %all_gather.6.join_hbm = bf16[192,2560]{1,0:T(8,128)(2,1)} all-gather(bf16[24,2560]{1,0:T(8,128)(2,1)S(1)} %get-tuple-element.14), channel_id=1, replica_groups=mesh['dp'=96,'tensor'=8] {'tensor'}, dimensions={0}, use_global_device_ids=true | all-gather | bytes 1105920 | tf_op jit(solution)/shard_map/all_gather | solution.py:406
  128.3 3.0 %shard_map.88 = bf16[768,128]{1,0:T(8,128)(2,1)S(1)} custom-call(bf16[192,2560]{1,0:T(8,128)(2,1)} %all_gather.6.join_hbm, bf16[448,2432]{1,0:T(8,128)(2,1)S(1)} %get-tuple-element.12.up_ref, bf16[448,2432]{1,0:T(8,128)(2,1)} %bitcast.29), custom_call_target="tpu_custom_call" | custom-call | tf_op jit(solution)/shard_map/pallas_call | solution.py:412
  131.3 39.3 %all_to_all.16 = bf16[96,8,128]{2,1,0:T(8,128)(2,1)S(1)} all-to-all(bf16[96,8,128]{2,1,0:T(8,128)(2,1)S(1)} %bitcast.22), channel_id=1, replica_groups=mesh['dp'=96,'tensor'=8] {'dp'}, dimensions={0} | all-to-all | bytes 393216 | tf_op jit(solution)/shard_map/all_to_all | solution.py:348
  170.6 0.0 all-gather.2.cloned.1.call-done.join_hbm
  170.6 0.0 copy-start.1
  170.6 0.0 copy-start.2
  170.6 3.4 %shard_map.89 = bf16[1536,128]{1,0:T(8,128)(2,1)S(1)} custom-call(bf16[192,4992]{1,0:T(8,128)(2,1)} %all-gather.2.cloned.1.call-done.join_hbm, bf16[448,2432]{1,0:T(8,128)(2,1)S(1)} %get-tuple-element.12.up_ref, bf16[448,2432]{1,0:T(8,128)(2,1)} %bitcast.30, bf16[768,128]{1,0:T(8,128)(2,1)S(1)} %bitcast.18), custom_call_target="tpu_custom_call" | custom-call | tf_op jit(solution)/shard_map/pallas_call | solution.py:426
  174.0 28.1 %all_to_all.17 = bf16[96,16,128]{2,1,0:T(8,128)(2,1)S(1)} all-to-all(bf16[96,16,128]{2,1,0:T(8,128)(2,1)S(1)} %bitcast.21), channel_id=1, replica_groups=mesh['dp'=96,'tensor'=8] {'dp'}, dimensions={0} | all-to-all | bytes 786432 | tf_op jit(solution)/shard_map/all_to_all | solution.py:348
  202.2 0.0 copy-done.1
  202.2 0.0 copy-done.2
  202.2 1.3 shard_map.90
Async XLA Ops:
  7.2 96.2 %reduce-scatter.2.cloned.1.call-start = ((), (), s32[]{:S(2)}) async-start(), calls=%async_computation.4 | async-start | bytes 3502080 | tf_op jit(solution)/shard_map/reduce_scatter | solution.py:394
  59.6 111.0 %all-gather.2.cloned.1.call-start = ((), (), s32[]{:S(2)}) async-start(), calls=%async_computation.5 | async-start | bytes 2156544 | tf_op jit(solution)/shard_map/all_gather | solution.py:405
  103.4 1.0 copy-start
  170.6 31.6 %copy-start.1 = (s32[128,2]{0,1:T(2,128)S(1)}, s32[128,2]{0,1:T(2,128)}, u32[]{:S(2)}) copy-start(s32[128,2]{0,1:T(2,128)} %param.8) | copy-start | bytes 3076
  170.6 31.6 %copy-start.2 = (f32[128,2]{0,1:T(2,128)S(1)}, f32[128,2]{0,1:T(2,128)}, u32[]{:S(2)}) copy-start(f32[128,2]{0,1:T(2,128)} %param.9) | copy-start | bytes 3076
Sparse Core Ops, SparseCore 0:
  59.7 43.6 reduce-scatter.1
  105.8 45.8 all-gather.1

commit v5 on v3

--- a/solution.py
+++ b/solution.py
@@ -335,6 +335,14 @@
     ).astype(BF16)
     grad_ref[...] = lax.dot_general(parts, either, along, preferred_element_type=F32).astype(BF16)
     score_ref[...] = jnp.concatenate(scores, axis=0) / probs_ref[...]
+
+
+def gather_by_pairs(rows, devices):
+    pairs = [[i, i + 1] for i in range(0, devices, 2)]
+    parities = [list(range(i, devices, 2)) for i in range(2)]
+    for groups in (pairs, parities):
+        rows = lax.all_gather(rows, "tensor", axis=0, tiled=True, axis_index_groups=groups)
+    return rows
 
 
 def in_hbm(array):
@@ -402,7 +410,7 @@
     )(share)
     whole = pl.BlockSpec(memory_space=pltpu.VMEM)
     joined = lax.all_gather(large, "tensor", axis=0, tiled=True)
-    joined_small = lax.all_gather(small, "tensor", axis=0, tiled=True)
+    joined_small = gather_by_pairs(small, devices)
     products = [
         pltpu.VMEM((2 * each * devices, feat), F32),
         pltpu.VMEM((2 * each * devices, feat), F32),

time: 209 us -> 208 us (level)
  starting transfers between devices: 23.6 us -> 20.5 us
  blocking collectives: 98.1 us -> 101 us
    all_to_all x1, starting transfers between devices: 23.5 us -> 20.5 us  [exchange(): block = lax.all_to_all(block, 'dp', split_axis=0, concat_axis=0, tiled=True)]
    all_gather x1 -> x2, blocking collectives: 22.9 us -> 25.8 us  [gather_by_pairs(): lax.all_gather(rows, 'tensor', axis=0, tiled=True, axis_index_groups=groups)]
where the time goes in v5:
time: 208 us
  blocking collectives  101 us (49%)
  waiting for transfers between devices  56.3 us (27%)
  starting transfers between devices  20.5 us (10%)
  Pallas kernels  14.7 us (7%)
  between operations  14.1 us (7%)
    all_to_all x2, blocking collectives, exchange(): block = lax.all_to_all(block, 'dp', split_axis=0, concat_axis=0, tiled=True)  75.3 us
    reduce_scatter x1, waiting for transfers between devices, per_device(): share = lax.psum_scatter(partial, 'tensor', scatter_dimension=0, tiled=True)  43.7 us
    all_gather x2, blocking collectives, gather_by_pairs(): lax.all_gather(rows, 'tensor', axis=0, tiled=True, axis_index_groups=groups)  25.8 us
    all_to_all x1, starting transfers between devices, exchange(): block = lax.all_to_all(block, 'dp', split_axis=0, concat_axis=0, tiled=True)  20.5 us
    all_to_all x1, waiting for transfers between devices, exchange(): block = lax.all_to_all(block, 'dp', split_axis=0, concat_axis=0, tiled=True)  12.5 us
  transfers between devices with their start and end apart: 3, of which 2 were waited for; matrix products, arithmetic and copies ran while one was open for 0% of the time, Pallas kernels for 3%

profile of v5, /device:TPU:1, one launch (start us, length us, event | category | flops | bytes accessed | tf_op | source)
XLA Modules:
  0.0 207.6 jit_solution(12640118669735726387)
XLA Ops:
  7.2 0.0 reduce-scatter.2.cloned.1.call-start
  7.2 2.5 %shard_map.85 = (bf16[2304,128]{1,0:T(8,128)(2,1)S(1)}, bf16[448,2432]{1,0:T(8,128)(2,1)S(1)}, bf16[448,2432]{1,0:T(8,128)(2,1)S(1)}) custom-call(s32[2,128]{1,0:T(2,128)} %bitcast.22, f32[2,128]{1,0:T(2,128)} %bitcast.24, bf16[448,128]{1,0:T(8,128)(2,1)} %bitcast.30, bf16[448,128]{1,0:T(8,128)(2,1)} %bitcast.31, bf16[448,2432]{1,0:T(8,128)(2,1)} %bitcast.29, ...), custom_call_target="tpu_custom_call" | custom-call | tf_op jit(solution)/shard_map/pallas_call | solution.py:368
  9.7 47.1 %all_to_all.15 = bf16[96,24,128]{2,1,0:T(8,128)(2,1)S(1)} all-to-all(bf16[96,24,128]{2,1,0:T(8,128)(2,1)S(1)} %bitcast.21), channel_id=1, replica_groups=mesh['dp'=96,'tensor'=8] {'dp'}, dimensions={0} | all-to-all | bytes 1179648 | tf_op jit(solution)/shard_map/all_to_all | solution.py:355
  56.8 2.7 %shard_map.86 = bf16[320,4864]{1,0:T(8,128)(2,1)} custom-call(bf16[2304,128]{1,0:T(8,128)(2,1)S(1)} %bitcast.17, bf16[448,2432]{1,0:T(8,128)(2,1)S(1)} %get-tuple-element.12.up_ref, bf16[448,2432]{1,0:T(8,128)(2,1)S(1)} %get-tuple-element.13.down_ref), custom_call_target="tpu_custom_call" | custom-call | tf_op jit(solution)/shard_map/pallas_call | solution.py:388
  59.6 0.0 reduce-scatter.2.cloned.1.call-update
  59.6 0.0 all-gather.2.cloned.1.call-start
  59.7 43.7 %reduce-scatter.2.cloned.1.call-done.sum_ref = bf16[40,4864]{1,0:T(8,128)(2,1)} async-done(((bf16[320,4864]{1,0:T(8,128)(2,1)}), bf16[40,4864]{1,0:T(8,128)(2,1)}) %reduce-scatter.2.cloned.1.call-update) | async-done | bytes 389136 | tf_op jit(solution)/shard_map/reduce_scatter | solution.py:401
  103.4 0.0 copy-start
  103.4 1.0 copy-done
  104.4 1.1 shard_map.87
  105.5 0.0 all-gather.2.cloned.1.call-update
  105.5 4.4 %all_gather.9 = bf16[48,2560]{1,0:T(8,128)(2,1)S(1)} all-gather(bf16[24,2560]{1,0:T(8,128)(2,1)S(1)} %get-tuple-element.14), channel_id=1, replica_groups={{0,1},{2,3},{4,5},{6,7},{8,9},{10,11},{12,13},{14,15},{16,17},{18,19},{..., dimensions={0}, use_global_device_ids=true | all-gather | bytes 368640 | tf_op jit(solution)/shard_map/all_gather | solution.py:344
  109.9 21.4 %all_gather.10.join_hbm = bf16[192,2560]{1,0:T(8,128)(2,1)} all-gather(bf16[48,2560]{1,0:T(8,128)(2,1)S(1)} %all_gather.9), channel_id=1, replica_groups={{0,2,4,6},{1,3,5,7},{8,10,12,14},{9,11,13,15},{16,18,20,22},{17,19,21,2..., dimensions={0}, use_global_device_ids=true | all-gather | bytes 1228800 | tf_op jit(solution)/shard_map/all_gather | solution.py:344
  131.3 3.6 %shard_map.88 = bf16[768,128]{1,0:T(8,128)(2,1)} custom-call(bf16[192,2560]{1,0:T(8,128)(2,1)} %all_gather.10.join_hbm, bf16[448,2432]{1,0:T(8,128)(2,1)S(1)} %get-tuple-element.12.up_ref, bf16[448,2432]{1,0:T(8,128)(2,1)} %bitcast.27), custom_call_target="tpu_custom_call" | custom-call | tf_op jit(solution)/shard_map/pallas_call | solution.py:419
  134.9 20.5 %all-to-all-start.1 = ((bf16[96,8,128]{2,1,0:T(8,128)(2,1)}), bf16[96,8,128]{2,1,0:T(8,128)(2,1)S(1)}, u32[]{:S(2)}, u32[]{:S(2)}) async-start(bf16[96,8,128]{2,1,0:T(8,128)(2,1)} %bitcast.9), calls=%async_computation.2 | async-start | bytes 393216 | tf_op jit(solution)/shard_map/all_to_all | solution.py:355
  155.4 0.0 copy-start.1
  155.4 0.0 copy-start.2
  155.4 0.0 all-gather.2.cloned.1.call-done.join_hbm
  155.4 3.4 %shard_map.89 = bf16[1536,128]{1,0:T(8,128)(2,1)S(1)} custom-call(bf16[192,4992]{1,0:T(8,128)(2,1)} %all-gather.2.cloned.1.call-done.join_hbm, bf16[448,2432]{1,0:T(8,128)(2,1)S(1)} %get-tuple-element.12.up_ref, bf16[448,2432]{1,0:T(8,128)(2,1)} %bitcast.28), custom_call_target="tpu_custom_call" | custom-call | tf_op jit(solution)/shard_map/pallas_call | solution.py:433
  158.8 12.5 %all-to-all-done.1 = bf16[96,8,128]{2,1,0:T(8,128)(2,1)S(1)} async-done(((bf16[96,8,128]{2,1,0:T(8,128)(2,1)}), bf16[96,8,128]{2,1,0:T(8,128)(2,1)S(1)}, u32[]{:S(2)}, u32[]{:S(2)}) %all-to-all-start.1) | async-done | bytes 196640 | tf_op jit(solution)/shard_map/all_to_all | solution.py:355
  171.3 28.1 %all_to_all.16 = bf16[96,16,128]{2,1,0:T(8,128)(2,1)S(1)} all-to-all(bf16[96,16,128]{2,1,0:T(8,128)(2,1)S(1)} %bitcast.18), channel_id=1, replica_groups=mesh['dp'=96,'tensor'=8] {'dp'}, dimensions={0} | all-to-all | bytes 786432 | tf_op jit(solution)/shard_map/all_to_all | solution.py:355
  199.5 0.0 copy-done.1
  199.5 0.0 copy-done.2
  199.5 1.3 shard_map.90
Async XLA Ops:
  7.2 96.2 %reduce-scatter.2.cloned.1.call-start = ((), (), s32[]{:S(2)}) async-start(), calls=%async_computation.4 | async-start | bytes 3502080 | tf_op jit(solution)/shard_map/reduce_scatter | solution.py:401
  59.6 95.8 %all-gather.2.cloned.1.call-start = ((), (), s32[]{:S(2)}) async-start(), calls=%async_computation.5 | async-start | bytes 2156544 | tf_op jit(solution)/shard_map/all_gather | solution.py:412
  103.4 1.0 copy-start
  134.9 36.4 %all-to-all-start.1 = ((bf16[96,8,128]{2,1,0:T(8,128)(2,1)}), bf16[96,8,128]{2,1,0:T(8,128)(2,1)S(1)}, u32[]{:S(2)}, u32[]{:S(2)}) async-start(bf16[96,8,128]{2,1,0:T(8,128)(2,1)} %bitcast.9), calls=%async_computation.2 | async-start | bytes 393216 | tf_op jit(solution)/shard_map/all_to_all | solution.py:355
  155.4 44.1 %copy-start.1 = (s32[128,2]{0,1:T(2,128)S(1)}, s32[128,2]{0,1:T(2,128)}, u32[]{:S(2)}) copy-start(s32[128,2]{0,1:T(2,128)} %param.8) | copy-start | bytes 3076
  155.4 44.1 %copy-start.2 = (f32[128,2]{0,1:T(2,128)S(1)}, f32[128,2]{0,1:T(2,128)}, u32[]{:S(2)}) copy-start(f32[128,2]{0,1:T(2,128)} %param.9) | copy-start | bytes 3076
Sparse Core Ops, SparseCore 0:
  59.7 43.6 reduce-scatter.1
  105.8 47.9 all-gather.1

commit v6 on v3

--- a/solution.py
+++ b/solution.py
@@ -68,11 +68,9 @@
     probs_hbm,
     tok_hbm,
     cot_hbm,
-    up_hbm,
-    down_hbm,
+    _up,
+    _down,
     out_ref,
-    up_ref,
-    down_ref,
     scratch,
     ids_ref,
     probs_ref,
@@ -82,11 +80,11 @@
 ):
     experts = out_ref.shape[0] // BLOCK
     started = copies(
-        (ids_hbm, probs_hbm, tok_hbm, cot_hbm, up_hbm, down_hbm),
-        (ids_ref, probs_ref, tok_ref, cot_ref, up_ref, down_ref),
+        (ids_hbm, probs_hbm, tok_hbm, cot_hbm),
+        (ids_ref, probs_ref, tok_ref, cot_ref),
         semaphores,
     )
-    for copy in started[:4]:
+    for copy in started:
         copy.wait()
     named, slot = one_hots(ids_ref, experts)
     either = named[0] + named[1]
@@ -103,8 +101,6 @@
     for r in range(7 * CAP, BLOCK):
         scratch[pl.ds(r, experts, stride=BLOCK), :] = jnp.zeros((experts, LANES), F32)
     out_ref[...] = scratch[...].astype(BF16)
-    for copy in started[4:]:
-        copy.wait()
 
 
 def row_of(device, slot, each):
@@ -211,13 +207,33 @@
 ):
     hidden = up_ref.shape[1]
     across = (((1,), (1,)), ((), ()))
-    started = copies((join_hbm, down_hbm), (join_ref, down_ref), semaphores)
-    started[0].wait()
-    joined = join_ref[:, :hidden]
-    part_rows[...] = lax.dot_general(joined, up_ref[...], across, preferred_element_type=F32)
+    spans = chunks(hidden, 1024)
+    own = [columns_at(at, to) for at, to in spans]
+    parts = own[:-1] + [columns_at(spans[-1][0], hidden + LANES)]
+    count = len(spans)
+    from_join = copies(
+        [join_hbm.at[part] for part in parts], [join_ref.at[part] for part in parts], semaphores
+    )
+    from_down = copies(
+        [down_hbm.at[part] for part in own],
+        [down_ref.at[part] for part in own],
+        semaphores.at[pl.ds(count, count)],
+    )
+    total = 0.0
+    for i in range(count):
+        from_join[i].wait()
+        total += lax.dot_general(
+            join_ref[own[i]], up_ref[own[i]], across, preferred_element_type=F32
+        )
+    part_rows[...] = total
     score_rows[...] = join_ref[:, hidden:].astype(F32)
-    started[1].wait()
-    out_rows[...] = lax.dot_general(joined, down_ref[...], across, preferred_element_type=F32)
+    total = 0.0
+    for i in range(count):
+        from_down[i].wait()
+        total += lax.dot_general(
+            join_ref[own[i]], down_ref[own[i]], across, preferred_element_type=F32
+        )
+    out_rows[...] = total
     each = join_ref.shape[0] // devices // 2
     pack(
         out_rows,
@@ -337,6 +353,10 @@
     score_ref[...] = jnp.concatenate(scores, axis=0) / probs_ref[...]
 
 
+def in_vmem(array):
+    return pltpu.with_memory_space_constraint(array, pltpu.VMEM)
+
+
 def in_hbm(array):
     return pltpu.with_memory_space_constraint(array, pltpu.HBM)
 
@@ -357,13 +377,9 @@
     packed = jax.ShapeDtypeStruct((experts * BLOCK, LANES), BF16)
     stage = [pltpu.VMEM((experts * BLOCK, LANES), F32)]
     anywhere = pl.BlockSpec(memory_space=pltpu.HBM)
-    send, up_near, down_near = pl.pallas_call(
+    send = pl.pallas_call(
         dispatch_kernel,
-        out_shape=(
-            packed,
-            pltpu.VMEM(up.shape, BF16),
-            pltpu.VMEM(down.shape, BF16),
-        ),
+        out_shape=packed,
         in_specs=[anywhere] * 6,
         scratch_shapes=stage
         + [
@@ -371,7 +387,7 @@
             pltpu.VMEM(probs.shape, F32),
             pltpu.VMEM((feat, count), BF16),
             pltpu.VMEM((feat, count), BF16),
-            pltpu.SemaphoreType.DMA((6,)),
+            pltpu.SemaphoreType.DMA((4,)),
         ],
         compiler_params=params(14),
     )(*map(in_hbm, (ids, probs, tokens.T, cotangent.T, up, down)))
@@ -389,7 +405,7 @@
             pltpu.SemaphoreType.DMA((2 * len(chunks(hidden, 512)),)),
         ],
         compiler_params=params(20),
-    )(exchange(send, experts), up_near, down_near)
+    )(exchange(send, experts), in_vmem(up), in_vmem(down))
     share = lax.psum_scatter(partial, "tensor", scatter_dimension=0, tiled=True)
     small, large = pl.pallas_call(
         middle_kernel,
@@ -418,9 +434,9 @@
             pltpu.VMEM(down.shape, BF16),
         ]
         + products
-        + [pltpu.SemaphoreType.DMA((2,))],
+        + [pltpu.SemaphoreType.DMA((2 * len(chunks(hidden, 1024)),))],
         compiler_params=params(20),
-    )(in_hbm(joined_small), up_near, in_hbm(down))
+    )(in_hbm(joined_small), up, in_hbm(down))
     back_small = exchange(back_small, experts)
     back = pl.pallas_call(
         functools.partial(down_large_kernel, devices),
@@ -434,7 +450,7 @@
         + products
         + [pltpu.SemaphoreType.DMA((3 * len(chunks(hidden, 1024)) + 1,))],
         compiler_params=params(20),
-    )(in_hbm(joined), up_near, in_hbm(down))
+    )(in_hbm(joined), up, in_hbm(down))
     mixed, input_grad, prob_grad = pl.pallas_call(
         combine_kernel,
         out_shape=(

time: 209 us -> 208 us (level)
  no operation moved by 1% of the time
where the time goes in v6:
time: 208 us; the launch traced here: 207 us
  blocking collectives  98.1 us (47%)
  waiting for transfers between devices  56.3 us (27%)
  starting transfers between devices  23.7 us (11%)
  Pallas kernels  14.2 us (7%)
  between operations  14.1 us (7%)
    all_to_all x2, blocking collectives, exchange(): block = lax.all_to_all(block, 'dp', split_axis=0, concat_axis=0, tiled=True)  75.3 us
    reduce_scatter x1, waiting for transfers between devices, per_device(): share = lax.psum_scatter(partial, 'tensor', scatter_dimension=0, tiled=True)  43.8 us
    all_to_all x1, starting transfers between devices, exchange(): block = lax.all_to_all(block, 'dp', split_axis=0, concat_axis=0, tiled=True)  23.7 us
    all_gather x1, blocking collectives, per_device(): joined_small = lax.all_gather(small, 'tensor', axis=0, tiled=True)  22.8 us
    all_to_all x1, waiting for transfers between devices, exchange(): block = lax.all_to_all(block, 'dp', split_axis=0, concat_axis=0, tiled=True)  12.5 us
  transfers between devices with their start and end apart: 3, of which 2 were waited for; matrix products, arithmetic and copies ran while one was open for 0% of the time, Pallas kernels for 3%

profile of v6, /device:TPU:1, one launch (start us, length us, event | category | flops | bytes accessed | tf_op | source)
XLA Modules:
  0.0 207.5 jit_solution(6525661057274472672)
XLA Ops:
  7.2 0.0 reduce-scatter.2.cloned.1.call-start
  7.2 0.0 copy-start
  7.2 0.0 copy-start.1
  7.2 1.8 shard_map.85
  9.1 47.1 %all_to_all.15 = bf16[96,24,128]{2,1,0:T(8,128)(2,1)S(1)} all-to-all(bf16[96,24,128]{2,1,0:T(8,128)(2,1)S(1)} %bitcast.25), channel_id=1, replica_groups=mesh['dp'=96,'tensor'=8] {'dp'}, dimensions={0} | all-to-all | bytes 1179648 | tf_op jit(solution)/shard_map/all_to_all | solution.py:367
  56.2 0.0 copy-done.1
  56.2 2.8 %shard_map.86 = bf16[320,4864]{1,0:T(8,128)(2,1)} custom-call(bf16[2304,128]{1,0:T(8,128)(2,1)S(1)} %bitcast.26, bf16[448,2432]{1,0:T(8,128)(2,1)S(1)} %bitcast.18, bf16[448,2432]{1,0:T(8,128)(2,1)S(1)} %bitcast.24), custom_call_target="tpu_custom_call" | custom-call | tf_op jit(solution)/shard_map/pallas_call | solution.py:396
  59.0 0.0 reduce-scatter.2.cloned.1.call-update
  59.0 0.0 all-gather.2.cloned.1.call-start
  59.0 43.8 %reduce-scatter.2.cloned.1.call-done.sum_ref = bf16[40,4864]{1,0:T(8,128)(2,1)} async-done(((bf16[320,4864]{1,0:T(8,128)(2,1)}), bf16[40,4864]{1,0:T(8,128)(2,1)}) %reduce-scatter.2.cloned.1.call-update) | async-done | bytes 389136 | tf_op jit(solution)/shard_map/reduce_scatter | solution.py:409
  102.8 1.0 copy-done.2
  103.8 1.0 shard_map.87
  104.9 0.0 all-gather.2.cloned.1.call-update
  104.9 22.8 %all_gather.6.join_hbm = bf16[192,2560]{1,0:T(8,128)(2,1)} all-gather(bf16[24,2560]{1,0:T(8,128)(2,1)S(1)} %get-tuple-element.8), channel_id=1, replica_groups=mesh['dp'=96,'tensor'=8] {'tensor'}, dimensions={0}, use_global_device_ids=true | all-gather | bytes 1105920 | tf_op jit(solution)/shard_map/all_gather | solution.py:421
  127.7 3.8 %shard_map.88 = bf16[768,128]{1,0:T(8,128)(2,1)} custom-call(bf16[192,2560]{1,0:T(8,128)(2,1)} %all_gather.6.join_hbm, bf16[448,2432]{1,0:T(8,128)(2,1)S(1)} %bitcast.19, bf16[448,2432]{1,0:T(8,128)(2,1)} %bitcast.22), custom_call_target="tpu_custom_call" | custom-call | tf_op jit(solution)/shard_map/pallas_call | solution.py:427
  131.5 23.7 %all-to-all-start.1 = ((bf16[96,8,128]{2,1,0:T(8,128)(2,1)}), bf16[96,8,128]{2,1,0:T(8,128)(2,1)S(1)}, u32[]{:S(2)}, u32[]{:S(2)}) async-start(bf16[96,8,128]{2,1,0:T(8,128)(2,1)} %bitcast.9), calls=%async_computation.2 | async-start | bytes 393216 | tf_op jit(solution)/shard_map/all_to_all | solution.py:367
  155.2 0.0 copy-start.3
  155.2 0.0 copy-start.4
  155.2 0.0 all-gather.2.cloned.1.call-done.join_hbm
  155.2 3.4 %shard_map.89 = bf16[1536,128]{1,0:T(8,128)(2,1)S(1)} custom-call(bf16[192,4992]{1,0:T(8,128)(2,1)} %all-gather.2.cloned.1.call-done.join_hbm, bf16[448,2432]{1,0:T(8,128)(2,1)S(1)} %bitcast.20, bf16[448,2432]{1,0:T(8,128)(2,1)} %bitcast.23), custom_call_target="tpu_custom_call" | custom-call | tf_op jit(solution)/shard_map/pallas_call | solution.py:441
  158.6 12.5 %all-to-all-done.1 = bf16[96,8,128]{2,1,0:T(8,128)(2,1)S(1)} async-done(((bf16[96,8,128]{2,1,0:T(8,128)(2,1)}), bf16[96,8,128]{2,1,0:T(8,128)(2,1)S(1)}, u32[]{:S(2)}, u32[]{:S(2)}) %all-to-all-start.1) | async-done | bytes 196640 | tf_op jit(solution)/shard_map/all_to_all | solution.py:367
  171.1 28.1 %all_to_all.16 = bf16[96,16,128]{2,1,0:T(8,128)(2,1)S(1)} all-to-all(bf16[96,16,128]{2,1,0:T(8,128)(2,1)S(1)} %bitcast.27), channel_id=1, replica_groups=mesh['dp'=96,'tensor'=8] {'dp'}, dimensions={0} | all-to-all | bytes 786432 | tf_op jit(solution)/shard_map/all_to_all | solution.py:367
  199.3 0.0 copy-done.4
  199.3 1.3 shard_map.90
  (3 shorter events, 0.0 us)
Async XLA Ops:
  7.2 95.7 %reduce-scatter.2.cloned.1.call-start = ((), (), s32[]{:S(2)}) async-start(), calls=%async_computation.4 | async-start | bytes 3502080 | tf_op jit(solution)/shard_map/reduce_scatter | solution.py:409
  7.2 49.0 %copy-start = (bf16[1,448,2432]{2,1,0:T(8,128)(2,1)S(1)}, bf16[1,448,2432]{2,1,0:T(8,128)(2,1)}, u32[]{:S(2)}) copy-start(bf16[1,448,2432]{2,1,0:T(8,128)(2,1)} %param.10) | copy-start | bytes 6537220
  7.2 49.0 %copy-start.1 = (bf16[1,2432,448]{1,2,0:T(8,128)(2,1)S(1)}, bf16[1,2432,448]{1,2,0:T(8,128)(2,1)}, u32[]{:S(2)}) copy-start(bf16[1,2432,448]{1,2,0:T(8,128)(2,1)} %param.11) | copy-start | bytes 6537220
  59.0 96.2 %all-gather.2.cloned.1.call-start = ((), (), s32[]{:S(2)}) async-start(), calls=%async_computation.5 | async-start | bytes 2156544 | tf_op jit(solution)/shard_map/all_gather | solution.py:420
  102.8 1.0 copy-start.2
  131.5 39.6 %all-to-all-start.1 = ((bf16[96,8,128]{2,1,0:T(8,128)(2,1)}), bf16[96,8,128]{2,1,0:T(8,128)(2,1)S(1)}, u32[]{:S(2)}, u32[]{:S(2)}) async-start(bf16[96,8,128]{2,1,0:T(8,128)(2,1)} %bitcast.9), calls=%async_computation.2 | async-start | bytes 393216 | tf_op jit(solution)/shard_map/all_to_all | solution.py:367
  155.2 44.1 %copy-start.3 = (s32[128,2]{0,1:T(2,128)S(1)}, s32[128,2]{0,1:T(2,128)}, u32[]{:S(2)}) copy-start(s32[128,2]{0,1:T(2,128)} %param.8) | copy-start | bytes 3076
  155.2 44.1 %copy-start.4 = (f32[128,2]{0,1:T(2,128)S(1)}, f32[128,2]{0,1:T(2,128)}, u32[]{:S(2)}) copy-start(f32[128,2]{0,1:T(2,128)} %param.9) | copy-start | bytes 3076
Sparse Core Ops, SparseCore 0:
  59.1 43.6 reduce-scatter.1
  105.2 46.2 all-gather.1

commit v7 on v6

--- a/solution.py
+++ b/solution.py
@@ -13,7 +13,6 @@
 SHARE = 40
 HEAD = 16
 SMALL = 8
-LARGE = 16
 F32 = jnp.float32
 BF16 = jnp.bfloat16
 MIB = 1024 * 1024
@@ -175,7 +174,11 @@
     return (slice(None), slice(at, to))
 
 
-def pack(out_ref, part_ref, scores, target, rows, devices, each, slots, height):
+def place(slot, j):
+    return slot * 7 + j if j < 7 else 7 * CAP + slot
+
+
+def pack(out_ref, part_ref, scores, target, rows, devices, each, slots, place, height):
     for d in range(devices):
         for s in range(slots):
             low, high = rows(d, s)
@@ -183,12 +186,10 @@
             right = slice(high, high + each)
             out, part = out_ref[left, :], part_ref[right, :]
             for j in range(7):
-                target[pl.ds(d * each * height + s * 7 + j, each, stride=height), :] = tile_of(
-                    out, part, j
-                )
-            target[pl.ds(d * each * height + 7 * slots + s, each, stride=height), :] = scores[
-                left, :
-            ]
+                at = d * each * height + place(s, j)
+                target[pl.ds(at, each, stride=height), :] = tile_of(out, part, j)
+            at = d * each * height + place(s, 7)
+            target[pl.ds(at, each, stride=height), :] = scores[left, :]
 
 
 def down_small_kernel(
@@ -244,6 +245,7 @@
         devices,
         each,
         1,
+        lambda s, j: j,
         SMALL,
     )
     out_ref[...] = target[...].astype(BF16)
@@ -254,8 +256,10 @@
     join_hbm,
     up_ref,
     down_hbm,
+    small_ref,
     out_ref,
     target,
+    small_rows,
     join_ref,
     down_ref,
     out_rows,
@@ -307,36 +311,42 @@
     def rows(d, s):
         return ((2 * d + s) * each,) * 2
 
+    sources = small_ref.shape[0] // SMALL
+    small_rows[...] = small_ref[...].astype(F32)
+    for j in range(SMALL):
+        target[pl.ds(place(0, j), sources, stride=BLOCK), :] = small_rows[
+            pl.ds(j, sources, stride=SMALL), :
+        ]
     pack(
-        out_rows, part_rows, score_rows, target, rows, devices, each, 2, LARGE
+        out_rows,
+        part_rows,
+        score_rows,
+        target,
+        rows,
+        devices,
+        each,
+        2,
+        lambda s, j: place(s + 1, j),
+        BLOCK,
     )
     out_ref[...] = target[...].astype(BF16)
 
 
-def combine_kernel(
-    ids_ref, probs_ref, small_ref, large_ref, mixed_ref, grad_ref, score_ref, first_rows, rest_rows
-):
-    experts = small_ref.shape[0] // SMALL
+def combine_kernel(ids_ref, probs_ref, block_ref, mixed_ref, grad_ref, score_ref, scratch):
+    experts = block_ref.shape[0] // BLOCK
     named, slot = one_hots(ids_ref, experts)
-    first_rows[...] = small_ref[...].astype(F32)
-    rest_rows[...] = large_ref[...].astype(F32)
-
-    def came(slot, j):
-        if slot == 0:
-            return first_rows[pl.ds(j, experts, stride=SMALL), :]
-        at = (slot - 1) * 7 + j if j < 7 else 14 + slot - 1
-        return rest_rows[pl.ds(at, experts, stride=LARGE), :]
-
+    scratch[...] = block_ref[...].astype(F32)
     along = (((0,), (0,)), ((), ()))
     outs, parts, picks = [], [], []
     scores = [jnp.zeros((1, ids_ref.shape[1]), F32) for _ in range(2)]
     for s in range(CAP):
         here = (slot == s).astype(F32)
-        first, second = pair_of([came(s, j) for j in range(7)])
+        tiles = [scratch[pl.ds(s * 7 + j, experts, stride=BLOCK), :] for j in range(7)]
+        first, second = pair_of(tiles)
         outs.append(first)
         parts.append(second)
         picks.append(jnp.concatenate([named[0] * here, named[1] * here], axis=1))
-        tail = came(s, 7)
+        tail = scratch[pl.ds(7 * CAP + s, experts, stride=BLOCK), :]
         value = tail[:, 0:1] + tail[:, 1:2]
         for k in range(2):
             scores[k] += jnp.sum(named[k] * here * value, axis=0, keepdims=True)
@@ -437,20 +447,20 @@
         + [pltpu.SemaphoreType.DMA((2 * len(chunks(hidden, 1024)),))],
         compiler_params=params(20),
     )(in_hbm(joined_small), up, in_hbm(down))
-    back_small = exchange(back_small, experts)
     back = pl.pallas_call(
         functools.partial(down_large_kernel, devices),
-        out_shape=jax.ShapeDtypeStruct((experts * LARGE, LANES), BF16),
-        in_specs=[anywhere, whole, anywhere],
+        out_shape=packed,
+        in_specs=[anywhere, whole, anywhere, whole],
         scratch_shapes=[
-            pltpu.VMEM((experts * LARGE, LANES), F32),
+            pltpu.VMEM((experts * BLOCK, LANES), F32),
+            pltpu.VMEM((experts * SMALL, LANES), F32),
             pltpu.VMEM(joined.shape, BF16),
             pltpu.VMEM(down.shape, BF16),
         ]
         + products
         + [pltpu.SemaphoreType.DMA((3 * len(chunks(hidden, 1024)) + 1,))],
         compiler_params=params(20),
-    )(in_hbm(joined), up, in_hbm(down))
+    )(in_hbm(joined), up, in_hbm(down), back_small)
     mixed, input_grad, prob_grad = pl.pallas_call(
         combine_kernel,
         out_shape=(
@@ -458,12 +468,9 @@
             jax.ShapeDtypeStruct((feat, count), BF16),
             jax.ShapeDtypeStruct((2, count), F32),
         ),
-        scratch_shapes=[
-            pltpu.VMEM((experts * SMALL, LANES), F32),
-            pltpu.VMEM((experts * LARGE, LANES), F32),
-        ],
+        scratch_shapes=stage,
         compiler_params=params(14),
-    )(ids, probs, back_small, exchange(back, experts))
+    )(ids, probs, exchange(back, experts))
     return mixed.T, input_grad.T, prob_grad.T
 
 

time: 208 us -> 208 us (level)
  starting transfers between devices: 23.7 us -> 0.08 us
  blocking collectives: 98.1 us -> 114 us
  waiting for transfers between devices: 56.3 us -> 64.4 us
    all_to_all x1 -> x0, starting transfers between devices: 23.7 us -> none  [exchange(): block = lax.all_to_all(block, 'dp', split_axis=0, concat_axis=0, tiled=True)]
    all_gather x1, waiting for transfers between devices: 0.02 us -> 20.6 us  [per_device(): joined = lax.all_gather(large, 'tensor', axis=0, tiled=True)]
    all_to_all x2, blocking collectives: 75.3 us -> 91.4 us  [exchange(): block = lax.all_to_all(block, 'dp', split_axis=0, concat_axis=0, tiled=True)]
    all_to_all x1 -> x0, waiting for transfers between devices: 12.5 us -> none  [exchange(): block = lax.all_to_all(block, 'dp', split_axis=0, concat_axis=0, tiled=True)]
  transfers between devices with their start and end apart: 3 -> 2, of which waited for: 2 -> 2; matrix products, arithmetic and copies ran while one was open for 0% -> 0% of each run, Pallas kernels for 3% -> 1%
where the time goes in v7:
time: 208 us; the launch traced here: 207 us
  blocking collectives  114 us (55%)
  waiting for transfers between devices  64.4 us (31%)
  between operations  14.1 us (7%)
  Pallas kernels  13.5 us (6%)
    all_to_all x2, blocking collectives, exchange(): block = lax.all_to_all(block, 'dp', split_axis=0, concat_axis=0, tiled=True)  91.4 us
    reduce_scatter x1, waiting for transfers between devices, per_device(): share = lax.psum_scatter(partial, 'tensor', scatter_dimension=0, tiled=True)  43.8 us
    all_gather x1, blocking collectives, per_device(): joined_small = lax.all_gather(small, 'tensor', axis=0, tiled=True)  22.8 us
    all_gather x1, waiting for transfers between devices, per_device(): joined = lax.all_gather(large, 'tensor', axis=0, tiled=True)  20.6 us
  transfers between devices with their start and end apart: 2, of which 2 were waited for; matrix products, arithmetic and copies ran while one was open for 0% of the time, Pallas kernels for 1%

profile of v7, /device:TPU:1, one launch (start us, length us, event | category | flops | bytes accessed | tf_op | source)
XLA Modules:
  0.0 207.4 jit_solution(5915967532126739289)
XLA Ops:
  7.2 0.0 reduce-scatter.2.cloned.1.call-start
  7.2 0.0 copy-start
  7.2 0.0 copy-start.1
  7.2 1.8 shard_map.85
  9.1 47.1 %all_to_all.10 = bf16[96,24,128]{2,1,0:T(8,128)(2,1)S(1)} all-to-all(bf16[96,24,128]{2,1,0:T(8,128)(2,1)S(1)} %bitcast.24), channel_id=1, replica_groups=mesh['dp'=96,'tensor'=8] {'dp'}, dimensions={0} | all-to-all | bytes 1179648 | tf_op jit(solution)/shard_map/all_to_all | solution.py:377
  56.2 0.0 copy-done
  56.2 0.0 copy-done.1
  56.2 2.8 %shard_map.86 = bf16[320,4864]{1,0:T(8,128)(2,1)} custom-call(bf16[2304,128]{1,0:T(8,128)(2,1)S(1)} %bitcast.26, bf16[448,2432]{1,0:T(8,128)(2,1)S(1)} %bitcast.16, bf16[448,2432]{1,0:T(8,128)(2,1)S(1)} %bitcast.22), custom_call_target="tpu_custom_call" | custom-call | tf_op jit(solution)/shard_map/pallas_call | solution.py:406
  59.0 0.0 reduce-scatter.2.cloned.1.call-update
  59.0 0.0 all-gather.2.cloned.1.call-start
  59.1 43.8 %reduce-scatter.2.cloned.1.call-done.sum_ref = bf16[40,4864]{1,0:T(8,128)(2,1)} async-done(((bf16[320,4864]{1,0:T(8,128)(2,1)}), bf16[40,4864]{1,0:T(8,128)(2,1)}) %reduce-scatter.2.cloned.1.call-update) | async-done | bytes 389136 | tf_op jit(solution)/shard_map/reduce_scatter | solution.py:419
  102.9 1.0 copy-done.2
  103.8 1.0 shard_map.87
  104.9 0.0 all-gather.2.cloned.1.call-update
  104.9 22.8 %all_gather.7.join_hbm = bf16[192,2560]{1,0:T(8,128)(2,1)} all-gather(bf16[24,2560]{1,0:T(8,128)(2,1)S(1)} %get-tuple-element.9), channel_id=1, replica_groups=mesh['dp'=96,'tensor'=8] {'tensor'}, dimensions={0}, use_global_device_ids=true | all-gather | bytes 1105920 | tf_op jit(solution)/shard_map/all_gather | solution.py:431
  127.7 3.1 %shard_map.88.small_ref = bf16[768,128]{1,0:T(8,128)(2,1)S(1)} custom-call(bf16[192,2560]{1,0:T(8,128)(2,1)} %all_gather.7.join_hbm, bf16[448,2432]{1,0:T(8,128)(2,1)S(1)} %bitcast.17, bf16[448,2432]{1,0:T(8,128)(2,1)} %bitcast.20), custom_call_target="tpu_custom_call" | custom-call | tf_op jit(solution)/shard_map/pallas_call | solution.py:437
  130.8 0.0 copy-start.3
  130.8 0.0 copy-start.4
  130.9 20.6 %all-gather.2.cloned.1.call-done.join_hbm = bf16[192,4992]{1,0:T(8,128)(2,1)} async-done(((bf16[24,4992]{1,0:T(8,128)(2,1)}), bf16[192,4992]{1,0:T(8,128)(2,1)}) %all-gather.2.cloned.1.call-update) | async-done | bytes 1916944 | tf_op jit(solution)/shard_map/all_gather | solution.py:430
  151.5 3.4 %shard_map.89 = bf16[2304,128]{1,0:T(8,128)(2,1)S(1)} custom-call(bf16[192,4992]{1,0:T(8,128)(2,1)} %all-gather.2.cloned.1.call-done.join_hbm, bf16[448,2432]{1,0:T(8,128)(2,1)S(1)} %bitcast.18, bf16[448,2432]{1,0:T(8,128)(2,1)} %bitcast.21, bf16[768,128]{1,0:T(8,128)(2,1)S(1)} %shard_map.88.small_ref), custom_call_target="tpu_custom_call" | custom-call | tf_op jit(solution)/shard_map/pallas_call | solution.py:450
  154.9 44.3 %all_to_all.11 = bf16[96,24,128]{2,1,0:T(8,128)(2,1)S(1)} all-to-all(bf16[96,24,128]{2,1,0:T(8,128)(2,1)S(1)} %bitcast.23), channel_id=1, replica_groups=mesh['dp'=96,'tensor'=8] {'dp'}, dimensions={0} | all-to-all | bytes 1179648 | tf_op jit(solution)/shard_map/all_to_all | solution.py:377
  199.2 0.0 copy-done.3
  199.2 0.0 copy-done.4
  199.2 1.3 shard_map.90
  (1 shorter events, 0.0 us)
Async XLA Ops:
  7.2 95.7 %reduce-scatter.2.cloned.1.call-start = ((), (), s32[]{:S(2)}) async-start(), calls=%async_computation.3 | async-start | bytes 3502080 | tf_op jit(solution)/shard_map/reduce_scatter | solution.py:419
  7.2 49.0 %copy-start = (bf16[1,448,2432]{2,1,0:T(8,128)(2,1)S(1)}, bf16[1,448,2432]{2,1,0:T(8,128)(2,1)}, u32[]{:S(2)}) copy-start(bf16[1,448,2432]{2,1,0:T(8,128)(2,1)} %param.10) | copy-start | bytes 6537220
  7.2 49.0 %copy-start.1 = (bf16[1,2432,448]{1,2,0:T(8,128)(2,1)S(1)}, bf16[1,2432,448]{1,2,0:T(8,128)(2,1)}, u32[]{:S(2)}) copy-start(bf16[1,2432,448]{1,2,0:T(8,128)(2,1)} %param.11) | copy-start | bytes 6537220
  59.0 92.5 %all-gather.2.cloned.1.call-start = ((), (), s32[]{:S(2)}) async-start(), calls=%async_computation.4 | async-start | bytes 2156544 | tf_op jit(solution)/shard_map/all_gather | solution.py:430
  102.9 1.0 copy-start.2
  130.8 68.4 %copy-start.3 = (s32[128,2]{0,1:T(2,128)S(1)}, s32[128,2]{0,1:T(2,128)}, u32[]{:S(2)}) copy-start(s32[128,2]{0,1:T(2,128)} %param.8) | copy-start | bytes 3076
  130.8 68.4 %copy-start.4 = (f32[128,2]{0,1:T(2,128)S(1)}, f32[128,2]{0,1:T(2,128)}, u32[]{:S(2)}) copy-start(f32[128,2]{0,1:T(2,128)} %param.9) | copy-start | bytes 3076
Sparse Core Ops, SparseCore 0:
  59.2 43.6 reduce-scatter.1
  105.2 46.2 all-gather.1

commit v8 on v6

--- a/solution.py
+++ b/solution.py
@@ -351,6 +351,14 @@
     ).astype(BF16)
     grad_ref[...] = lax.dot_general(parts, either, along, preferred_element_type=F32).astype(BF16)
     score_ref[...] = jnp.concatenate(scores, axis=0) / probs_ref[...]
+
+
+def gather_by_pairs(rows, devices):
+    pairs = [[i, i + 1] for i in range(0, devices, 2)]
+    parities = [list(range(i, devices, 2)) for i in range(2)]
+    for groups in (pairs, parities):
+        rows = lax.all_gather(rows, "tensor", axis=0, tiled=True, axis_index_groups=groups)
+    return rows
 
 
 def in_vmem(array):
@@ -418,7 +426,7 @@
     )(share)
     whole = pl.BlockSpec(memory_space=pltpu.VMEM)
     joined = lax.all_gather(large, "tensor", axis=0, tiled=True)
-    joined_small = lax.all_gather(small, "tensor", axis=0, tiled=True)
+    joined_small = gather_by_pairs(small, devices)
     products = [
         pltpu.VMEM((2 * each * devices, feat), F32),
         pltpu.VMEM((2 * each * devices, feat), F32),

time: 208 us -> 208 us (level)
  starting transfers between devices: 23.7 us -> 20.7 us
  blocking collectives: 98.1 us -> 101 us
    all_to_all x1, starting transfers between devices: 23.7 us -> 20.6 us  [exchange(): block = lax.all_to_all(block, 'dp', split_axis=0, concat_axis=0, tiled=True)]
    all_gather x1 -> x2, blocking collectives: 22.8 us -> 25.8 us  [gather_by_pairs(): lax.all_gather(rows, 'tensor', axis=0, tiled=True, axis_index_groups=groups)]
where the time goes in v8:
time: 208 us; the launch traced here: 207 us
  blocking collectives  101 us (49%)
  waiting for transfers between devices  56.3 us (27%)
  starting transfers between devices  20.7 us (10%)
  Pallas kernels  14.2 us (7%)
  between operations  14.1 us (7%)
    all_to_all x2, blocking collectives, exchange(): block = lax.all_to_all(block, 'dp', split_axis=0, concat_axis=0, tiled=True)  75.3 us
    reduce_scatter x1, waiting for transfers between devices, per_device(): share = lax.psum_scatter(partial, 'tensor', scatter_dimension=0, tiled=True)  43.8 us
    all_gather x2, blocking collectives, gather_by_pairs(): lax.all_gather(rows, 'tensor', axis=0, tiled=True, axis_index_groups=groups)  25.8 us
    all_to_all x1, starting transfers between devices, exchange(): block = lax.all_to_all(block, 'dp', split_axis=0, concat_axis=0, tiled=True)  20.6 us
    all_to_all x1, waiting for transfers between devices, exchange(): block = lax.all_to_all(block, 'dp', split_axis=0, concat_axis=0, tiled=True)  12.5 us
  transfers between devices with their start and end apart: 3, of which 2 were waited for; matrix products, arithmetic and copies ran while one was open for 0% of the time, Pallas kernels for 3%

profile of v8, /device:TPU:1, one launch (start us, length us, event | category | flops | bytes accessed | tf_op | source)
XLA Modules:
  0.0 207.4 jit_solution(1598280129289212459)
XLA Ops:
  7.2 0.0 reduce-scatter.2.cloned.1.call-start
  7.2 0.0 copy-start
  7.2 0.0 copy-start.1
  7.2 1.8 shard_map.85
  9.1 47.1 %all_to_all.15 = bf16[96,24,128]{2,1,0:T(8,128)(2,1)S(1)} all-to-all(bf16[96,24,128]{2,1,0:T(8,128)(2,1)S(1)} %bitcast.25), channel_id=1, replica_groups=mesh['dp'=96,'tensor'=8] {'dp'}, dimensions={0} | all-to-all | bytes 1179648 | tf_op jit(solution)/shard_map/all_to_all | solution.py:375
  56.2 0.0 copy-done
  56.2 2.8 %shard_map.86 = bf16[320,4864]{1,0:T(8,128)(2,1)} custom-call(bf16[2304,128]{1,0:T(8,128)(2,1)S(1)} %bitcast.26, bf16[448,2432]{1,0:T(8,128)(2,1)S(1)} %bitcast.18, bf16[448,2432]{1,0:T(8,128)(2,1)S(1)} %bitcast.24), custom_call_target="tpu_custom_call" | custom-call | tf_op jit(solution)/shard_map/pallas_call | solution.py:404
  59.0 0.0 reduce-scatter.2.cloned.1.call-update
  59.0 0.0 all-gather.2.cloned.1.call-start
  59.0 43.8 %reduce-scatter.2.cloned.1.call-done.sum_ref = bf16[40,4864]{1,0:T(8,128)(2,1)} async-done(((bf16[320,4864]{1,0:T(8,128)(2,1)}), bf16[40,4864]{1,0:T(8,128)(2,1)}) %reduce-scatter.2.cloned.1.call-update) | async-done | bytes 389136 | tf_op jit(solution)/shard_map/reduce_scatter | solution.py:417
  102.8 1.0 copy-done.2
  103.8 1.0 shard_map.87
  104.9 0.0 all-gather.2.cloned.1.call-update
  104.9 4.4 %all_gather.9 = bf16[48,2560]{1,0:T(8,128)(2,1)S(1)} all-gather(bf16[24,2560]{1,0:T(8,128)(2,1)S(1)} %get-tuple-element.8), channel_id=1, replica_groups={{0,1},{2,3},{4,5},{6,7},{8,9},{10,11},{12,13},{14,15},{16,17},{18,19},{..., dimensions={0}, use_global_device_ids=true | all-gather | bytes 368640 | tf_op jit(solution)/shard_map/all_gather | solution.py:360
  109.3 21.4 %all_gather.10.join_hbm = bf16[192,2560]{1,0:T(8,128)(2,1)} all-gather(bf16[48,2560]{1,0:T(8,128)(2,1)S(1)} %all_gather.9), channel_id=1, replica_groups={{0,2,4,6},{1,3,5,7},{8,10,12,14},{9,11,13,15},{16,18,20,22},{17,19,21,2..., dimensions={0}, use_global_device_ids=true | all-gather | bytes 1228800 | tf_op jit(solution)/shard_map/all_gather | solution.py:360
  130.7 3.8 %shard_map.88 = bf16[768,128]{1,0:T(8,128)(2,1)} custom-call(bf16[192,2560]{1,0:T(8,128)(2,1)} %all_gather.10.join_hbm, bf16[448,2432]{1,0:T(8,128)(2,1)S(1)} %bitcast.19, bf16[448,2432]{1,0:T(8,128)(2,1)} %bitcast.22), custom_call_target="tpu_custom_call" | custom-call | tf_op jit(solution)/shard_map/pallas_call | solution.py:435
  134.5 20.6 %all-to-all-start.1 = ((bf16[96,8,128]{2,1,0:T(8,128)(2,1)}), bf16[96,8,128]{2,1,0:T(8,128)(2,1)S(1)}, u32[]{:S(2)}, u32[]{:S(2)}) async-start(bf16[96,8,128]{2,1,0:T(8,128)(2,1)} %bitcast.9), calls=%async_computation.2 | async-start | bytes 393216 | tf_op jit(solution)/shard_map/all_to_all | solution.py:375
  155.1 0.0 copy-start.3
  155.1 0.0 copy-start.4
  155.1 0.0 all-gather.2.cloned.1.call-done.join_hbm
  155.1 3.4 %shard_map.89 = bf16[1536,128]{1,0:T(8,128)(2,1)S(1)} custom-call(bf16[192,4992]{1,0:T(8,128)(2,1)} %all-gather.2.cloned.1.call-done.join_hbm, bf16[448,2432]{1,0:T(8,128)(2,1)S(1)} %bitcast.20, bf16[448,2432]{1,0:T(8,128)(2,1)} %bitcast.23), custom_call_target="tpu_custom_call" | custom-call | tf_op jit(solution)/shard_map/pallas_call | solution.py:449
  158.6 12.5 %all-to-all-done.1 = bf16[96,8,128]{2,1,0:T(8,128)(2,1)S(1)} async-done(((bf16[96,8,128]{2,1,0:T(8,128)(2,1)}), bf16[96,8,128]{2,1,0:T(8,128)(2,1)S(1)}, u32[]{:S(2)}, u32[]{:S(2)}) %all-to-all-start.1) | async-done | bytes 196640 | tf_op jit(solution)/shard_map/all_to_all | solution.py:375
  171.1 28.1 %all_to_all.16 = bf16[96,16,128]{2,1,0:T(8,128)(2,1)S(1)} all-to-all(bf16[96,16,128]{2,1,0:T(8,128)(2,1)S(1)} %bitcast.27), channel_id=1, replica_groups=mesh['dp'=96,'tensor'=8] {'dp'}, dimensions={0} | all-to-all | bytes 786432 | tf_op jit(solution)/shard_map/all_to_all | solution.py:375
  199.2 1.3 shard_map.90
  (4 shorter events, 0.0 us)
Async XLA Ops:
  7.2 95.7 %reduce-scatter.2.cloned.1.call-start = ((), (), s32[]{:S(2)}) async-start(), calls=%async_computation.4 | async-start | bytes 3502080 | tf_op jit(solution)/shard_map/reduce_scatter | solution.py:417
  7.2 49.0 %copy-start = (bf16[1,448,2432]{2,1,0:T(8,128)(2,1)S(1)}, bf16[1,448,2432]{2,1,0:T(8,128)(2,1)}, u32[]{:S(2)}) copy-start(bf16[1,448,2432]{2,1,0:T(8,128)(2,1)} %param.10) | copy-start | bytes 6537220
  7.2 49.0 %copy-start.1 = (bf16[1,2432,448]{1,2,0:T(8,128)(2,1)S(1)}, bf16[1,2432,448]{1,2,0:T(8,128)(2,1)}, u32[]{:S(2)}) copy-start(bf16[1,2432,448]{1,2,0:T(8,128)(2,1)} %param.11) | copy-start | bytes 6537220
  59.0 96.1 %all-gather.2.cloned.1.call-start = ((), (), s32[]{:S(2)}) async-start(), calls=%async_computation.5 | async-start | bytes 2156544 | tf_op jit(solution)/shard_map/all_gather | solution.py:428
  102.8 1.0 copy-start.2
  134.5 36.6 %all-to-all-start.1 = ((bf16[96,8,128]{2,1,0:T(8,128)(2,1)}), bf16[96,8,128]{2,1,0:T(8,128)(2,1)S(1)}, u32[]{:S(2)}, u32[]{:S(2)}) async-start(bf16[96,8,128]{2,1,0:T(8,128)(2,1)} %bitcast.9), calls=%async_computation.2 | async-start | bytes 393216 | tf_op jit(solution)/shard_map/all_to_all | solution.py:375
  155.1 44.1 %copy-start.3 = (s32[128,2]{0,1:T(2,128)S(1)}, s32[128,2]{0,1:T(2,128)}, u32[]{:S(2)}) copy-start(s32[128,2]{0,1:T(2,128)} %param.8) | copy-start | bytes 3076
  155.1 44.1 %copy-start.4 = (f32[128,2]{0,1:T(2,128)S(1)}, f32[128,2]{0,1:T(2,128)}, u32[]{:S(2)}) copy-start(f32[128,2]{0,1:T(2,128)} %param.9) | copy-start | bytes 3076
Sparse Core Ops, SparseCore 0:
  59.1 43.6 reduce-scatter.1
  105.2 48.9 all-gather.1
